TPU v7x, 128 devices: a whole 4x4x4 slice. The times are simulated.
128 devices in a mesh: lat: 4 (over x_hi, core), lon: 32 (over y, z, x_lo).
Axes of the slice: x: 4 (x_hi: 2, x_lo: 2; x = x_hi * 2 + x_lo), y: 4, z: 4, core: 2. Of those that a mesh axis runs over, the one named last changes fastest.
Arguments:
- tokens: bfloat16 [2, 768, 384, 512], P(None, 'lat', 'lon'), may hold values from -6 to 6
- region: int32 [2, 768, 384], P(None, 'lat', 'lon'), may hold values from 0 to 2
- w_qkv: bfloat16 [512, 1536], replicated, may hold values from -15 to 15
- w_out: bfloat16 [512, 512], replicated, may hold values from -0.25 to 0.25
- w_merge: bfloat16 [2048, 1024], replicated, may hold values from -0.125 to 0.125
Outputs:
- merged: bfloat16 [2, 384, 192, 1024], P(None, ('lat', 'lon'))
All inputs are finite; a program needn't handle non-finite values.
Results may differ from a plain program's by a relative error of at most 0.015.
Values may be sent and summed in bfloat16 or wider, within the bound.
A program may use at most 384 MiB of HBM per device.

v0:
```python
import jax
import jax.numpy as jnp
from jax import lax
from jax.sharding import PartitionSpec as P

HEADS = 16
WIN_LAT = 6
WIN_LON = 12


def shifted(value, axis, steps):
    count = lax.axis_size(axis)
    pairs = [(source, (source + steps) % count) for source in range(count)]
    return lax.ppermute(value, axis, pairs)


def normalize(values):
    center = values - jnp.mean(values, -1, keepdims=True)
    spread = jnp.mean(center * center, -1, keepdims=True)
    return center * lax.rsqrt(spread + 1e-05)


def attend_tile(tile, labels, w_qkv):
    level_count, row_count, column_count, channels = tile.shape
    head_size = channels // HEADS
    row_windows = row_count // WIN_LAT
    col_windows = column_count // WIN_LON
    window_count = row_windows * col_windows
    window_span = level_count * WIN_LAT * WIN_LON
    ordered = tile.reshape(level_count, row_windows, WIN_LAT, col_windows, WIN_LON, channels)
    ordered = ordered.transpose(1, 3, 0, 2, 4, 5).reshape(window_count * window_span, channels)
    normed = normalize(ordered.astype(jnp.float32)).astype(jnp.bfloat16)
    packed = jnp.dot(normed, w_qkv, preferred_element_type=jnp.float32).astype(jnp.bfloat16)
    window_labels = labels.reshape(level_count, row_windows, WIN_LAT, col_windows, WIN_LON)
    window_labels = window_labels.transpose(1, 3, 0, 2, 4).reshape(window_count, window_span)
    group_count = max(1, -(-window_count // 16))
    while window_count % group_count != 0:
        group_count = group_count + 1
    per_group = window_count // group_count
    packed = packed.reshape(group_count, per_group, window_span, 3, HEADS, head_size)
    window_labels = window_labels.reshape(group_count, per_group, window_span)
    score_scale = head_size ** (-0.5)

    def one_group(group_parts):
        group_packed, group_labels = group_parts
        queries = group_packed[:, :, 0]
        keys_in = group_packed[:, :, 1]
        values_in = group_packed[:, :, 2]
        allowed = group_labels[:, None, :, None] == group_labels[:, None, None, :]
        scores = (
            jnp.einsum("wqhd,wkhd->whqk", queries, keys_in, preferred_element_type=jnp.float32)
            * score_scale
        )
        scores = jnp.where(allowed, scores, -1e30)
        peak_score = jnp.max(scores, -1, keepdims=True)
        weights = jnp.exp(scores - peak_score)
        weights = (weights / jnp.sum(weights, -1, keepdims=True)).astype(jnp.bfloat16)
        result = jnp.einsum(
            "whqk,wkhd->wqhd", weights, values_in, preferred_element_type=jnp.float32
        )
        return result.astype(jnp.bfloat16).reshape(per_group, window_span, channels)

    mixed_out = lax.map(one_group, (packed, window_labels))
    mixed_out = mixed_out.reshape(row_windows, col_windows, level_count, WIN_LAT, WIN_LON, channels)
    return mixed_out.transpose(2, 0, 3, 1, 4, 5).reshape(
        level_count, row_count, column_count, channels
    )


def body(tokens, region, w_qkv, w_out, w_merge):
    level_count, row_count, column_count, channels = tokens.shape
    half_lat = WIN_LAT // 2
    half_lon = WIN_LON // 2
    region_marks = region.astype(jnp.bfloat16)
    after_rows = shifted((tokens[:, :half_lat], region_marks[:, :half_lat]), "lat", -1)
    tile = jnp.concatenate([tokens[:, half_lat:], after_rows[0]], axis=1)
    tile_marks = jnp.concatenate([region_marks[:, half_lat:], after_rows[1]], axis=1)
    after_cols = shifted((tile[:, :, :half_lon], tile_marks[:, :, :half_lon]), "lon", -1)
    tile = jnp.concatenate([tile[:, :, half_lon:], after_cols[0]], axis=2)
    tile_marks = jnp.concatenate([tile_marks[:, :, half_lon:], after_cols[1]], axis=2)
    total_rows = row_count * lax.axis_size("lat")
    global_row = (
        lax.axis_index("lat") * row_count + jnp.arange(tile.shape[1], dtype=jnp.int32) + half_lat
    ) % total_rows
    pole_side = (global_row < half_lat).astype(jnp.float32)
    labels = tile_marks.astype(jnp.float32) * 2.0 + pole_side[None, :, None]
    mixed_out = attend_tile(tile, labels, w_qkv)
    back_cols = shifted(mixed_out[:, :, column_count - half_lon :], "lon", 1)
    mixed_out = jnp.concatenate([back_cols, mixed_out[:, :, : column_count - half_lon]], axis=2)
    back_rows = shifted(mixed_out[:, row_count - half_lat :], "lat", 1)
    mixed_out = jnp.concatenate([back_rows, mixed_out[:, : row_count - half_lat]], axis=1)
    attended = jnp.dot(mixed_out.reshape(-1, channels), w_out, preferred_element_type=jnp.float32)
    updated = (tokens.astype(jnp.float32) + attended.reshape(tokens.shape)).astype(jnp.bfloat16)
    grouped = updated.reshape(level_count, row_count // 2, 2, column_count // 2, 2, channels)
    grouped = grouped.transpose(0, 1, 3, 2, 4, 5).reshape(
        level_count, row_count // 2, column_count // 2, 4 * channels
    )
    merge_in = normalize(grouped.astype(jnp.float32)).astype(jnp.bfloat16)
    merged = jnp.dot(
        merge_in.reshape(-1, 4 * channels), w_merge, preferred_element_type=jnp.float32
    )
    merged = merged.astype(jnp.bfloat16).reshape(
        level_count, row_count // 2, column_count // 2, 2 * channels
    )
    return lax.all_to_all(merged, "lon", split_axis=1, concat_axis=2, tiled=True)


def solution(mesh):
    in_specs = (P(None, "lat", "lon", None), P(None, "lat", "lon"), P(), P(), P())
    out_specs = P(None, ("lat", "lon"), None, None)
    return jax.shard_map(body, mesh=mesh, in_specs=in_specs, out_specs=out_specs, check_vma=False)
```

profile of v0, /device:TPU:0, one launch (start us, length us, event | category | flops | bytes accessed | tf_op | source)
XLA Modules:
  0.0 561.8 jit_solution(18234653912578307431)
XLA Ops:
  19.5 48.7 %collective-permute-done.2 = bf16[2,3,12]{1,0,2:T(2,128)(2,1)S(1)} collective-permute-done((bf16[2,3,12]{1,0,2:T(2,128)(2,1)S(1)}, bf16[2,3,12]{1,0,2:T(2,128)(2,1)S(1)}, u32[]{:S(2)}, u32[]{:S(2)}) %collective-permute-start.2) | collective-permute-done | bytes 176 | tf_op jit(solution)/shard_map/ppermute | solution.py:14
  75.8 15.3 %copy.47 = f32[2,192,12,512]{3,0,2,1:T(2,128)} copy(f32[2,192,12,512]{3,1,2,0:T(8,128)S(1)} %maximum_convert_fusion) | data formatting | bytes 18874368 | tf_op jit(solution)/shard_map/convert_element_type | solution.py:32
  91.1 9.4 %reduce_sum.45 = f32[32,2,6,12]{1,3,2,0:T(8,128)} reduce(f32[32,1,2,6,12,512]{5,2,4,3,0,1:T(2,128)} %bitcast.91, f32[]{:T(128)} %constant.50.clone.1), dimensions={1,5}, to_apply=%region_0.1 | reduce | flops 2354688 | bytes 9455620 | tf_op jit(solution)/shard_map/reduce_sum | solution.py:18
  102.0 11.6 %multiply_reduce_fusion.1 = f32[32,2,6,12]{1,3,2,0:T(8,128)} fusion(f32[32,1,2,6,12,512]{5,2,4,3,0,1:T(2,128)} %bitcast.92, f32[32,2,6,12]{1,3,2,0:T(8,128)S(1)} %broadcast_multiply_fusion), kind=kLoop, calls=%fused_computation.28 | loop fusion | flops 7073280 | bytes 9474048 | tf_op jit(solution)/shard_map/reduce_sum | solution.py:19
  115.2 10.7 %copy.48 = f32[32,1,2,6,12,512]{5,4,3,2,0,1:T(8,128)} copy(f32[32,1,2,6,12,512]{5,2,4,3,0,1:T(2,128)} %bitcast.93) | data formatting | bytes 18874368 | tf_op jit(solution)/shard_map/convert_element_type | solution.py:32
  129.7 11.7 %reshape.166 = f32[4608,512]{1,0:T(8,128)} reshape(f32[32,1,2,6,12,512]{5,4,3,2,0,1:T(8,128)} %copy.48) | data formatting | bytes 18874368 | tf_op jit(solution)/shard_map/convert_element_type | solution.py:32
  141.4 14.0 %convolution_convert_fusion = bf16[4608,1536]{1,0:T(8,128)(2,1)} fusion(bf16[512,1536]{1,0:T(8,128)(2,1)S(1)} %copy-done, f32[4608,512]{1,0:T(8,128)} %reshape.166, f32[4608]{0:T(1024)S(1)} %rsqrt.23, f32[4608]{0:T(1024)S(1)} %div.25), kind=kOutput, calls=%fused_computation.22 | convolution fusion | flops 7261913088 | bytes 25202688 | tf_op jit(solution)/shard_map/dot_general | solution.py:33
  155.4 18.8 %copy.54 = bf16[4608,1536]{0,1:T(8,128)(2,1)} copy(bf16[4608,1536]{1,0:T(8,128)(2,1)} %convolution_convert_fusion) | data formatting | bytes 28311552 | tf_op jit(solution)/shard_map/convert_element_type | solution.py:33
  174.2 44.4 %reshape.162 = bf16[2,16,144,3,16,32]{2,1,0,5,4,3:T(8,128)(2,1)} reshape(bf16[4608,1536]{0,1:T(8,128)(2,1)} %copy.54) | data formatting | bytes 28311552 | tf_op jit(solution)/shard_map/reshape | solution.py:40
  218.6 126.0 %while.10 = (s32[]{:T(128)}, bf16[2,16,144,512]{3,1,0,2:T(8,128)(2,1)}, bf16[2,16,144,3,16,32]{2,1,0,5,4,3:T(8,128)(2,1)}, f32[2,16,144]{2,1,0:T(8,128)S(1)}, s32[]{:T(128)}) while((s32[]{:T(128)}, bf16[2,16,144,512]{3,1,0,2:T(8,128)(2,1)}, bf16[2,16,144,3,16,32]{2,1,0,5,4,3:T(8,128)(2,1)}, f32[2,16,144]{2,1,0:T(8,128)S(1)}, s32[]{:T(128)}) %tuple.28), condition=%wide.region_5.6_spmd, body=%wide.region_2.5_spmd.sunk | while | flops 712839296 | bytes 112660032 | solution.py:63
  225.1 9.4 %copy.92 = bf16[1,16,144,3,16,32]{2,5,4,1,3,0:T(8,128)(2,1)} copy(bf16[1,16,144,3,16,32]{2,1,0,5,4,3:T(8,128)(2,1)S(1)} %constant_dynamic-slice_fusion.2) | data formatting | bytes 14155776 | tf_op jit(solution)/shard_map/while/body/jit(dynamic_index_in_dim)/dynamic_slice | solution.py:63
  234.9 19.9 %fusion.41 = (f32[16,16,144]{2,1,0:T(8,128)S(1)}, f32[16,16,144,144]{2,3,1,0:T(8,128)}) fusion(pred[16,144,144]{1,2,0:T(8,128)(4,1)S(1)} %broadcast_compare_fusion.2, bf16[16,144,3,16,32]{1,4,3,0,2:T(8,128)(2,1)} %bitcast.89), kind=kOutput, calls=%fused_computation.66.clone.1 | convolution fusion | flops 360972416 | bytes 30101504 | tf_op jit(solution)/shard_map/while/body/eval_jaxpr/sub | solution.py:56
  254.8 16.5 %fusion.42 = bf16[16,16,32,144]{3,2,1,0:T(8,128)(2,1)} fusion(f32[16,16,144,144]{2,3,1,0:T(8,128)} %get-tuple-element.87, f32[16,16,144]{2,1,0:T(8,128)S(1)} %get-tuple-element.88, bf16[16,144,3,16,32]{1,4,3,0,2:T(8,128)(2,1)} %bitcast.90), kind=kOutput, calls=%fused_computation.15.clone.1 | convolution fusion | flops 351535104 | bytes 44449792 | tf_op jit(solution)/shard_map/while/body/eval_jaxpr/whqk,wkhd->wqhd/dot_general | solution.py:58
  288.0 9.4 %copy.92 = bf16[1,16,144,3,16,32]{2,5,4,1,3,0:T(8,128)(2,1)} copy(bf16[1,16,144,3,16,32]{2,1,0,5,4,3:T(8,128)(2,1)S(1)} %constant_dynamic-slice_fusion.2) | data formatting | bytes 14155776 | tf_op jit(solution)/shard_map/while/body/jit(dynamic_index_in_dim)/dynamic_slice | solution.py:63
  297.8 19.9 %fusion.41 = (f32[16,16,144]{2,1,0:T(8,128)S(1)}, f32[16,16,144,144]{2,3,1,0:T(8,128)}) fusion(pred[16,144,144]{1,2,0:T(8,128)(4,1)S(1)} %broadcast_compare_fusion.2, bf16[16,144,3,16,32]{1,4,3,0,2:T(8,128)(2,1)} %bitcast.89), kind=kOutput, calls=%fused_computation.66.clone.1 | convolution fusion | flops 360972416 | bytes 30101504 | tf_op jit(solution)/shard_map/while/body/eval_jaxpr/sub | solution.py:56
  317.7 16.5 %fusion.42 = bf16[16,16,32,144]{3,2,1,0:T(8,128)(2,1)} fusion(f32[16,16,144,144]{2,3,1,0:T(8,128)} %get-tuple-element.87, f32[16,16,144]{2,1,0:T(8,128)S(1)} %get-tuple-element.88, bf16[16,144,3,16,32]{1,4,3,0,2:T(8,128)(2,1)} %bitcast.90), kind=kOutput, calls=%fused_computation.15.clone.1 | convolution fusion | flops 351535104 | bytes 44449792 | tf_op jit(solution)/shard_map/while/body/eval_jaxpr/whqk,wkhd->wqhd/dot_general | solution.py:58
  360.1 57.5 %collective-permute-done.4 = bf16[2,192,6,512]{3,1,2,0:T(8,128)(2,1)S(1)} collective-permute-done((bf16[2,192,6,512]{3,1,2,0:T(8,128)(2,1)S(1)}, bf16[2,192,6,512]{3,1,2,0:T(8,128)(2,1)S(1)}, u32[]{:S(2)}, u32[]{:S(2)}) %collective-permute-start.4) | collective-permute-done | bytes 2359328 | tf_op jit(solution)/shard_map/ppermute | solution.py:14
  429.7 12.4 %reshape.171 = f32[2,96,2,6,2,512]{5,2,1,4,3,0:T(2,128)} reshape(f32[2,192,12,512]{3,1,2,0:T(8,128)} %fusion.12) | data formatting | bytes 18874368 | tf_op jit(solution)/shard_map/convert_element_type | solution.py:98
  442.1 12.0 %fusion.34 = f32[2,96,6]{2,1,0:T(8,128)S(1)} fusion(f32[2,96,2,6,2,512]{5,2,1,4,3,0:T(2,128)} %reshape.171), kind=kLoop, calls=%fused_computation.65 | loop fusion | flops 2358144 | bytes 9441792 | tf_op jit(solution)/shard_map/reduce_sum | solution.py:18
  454.1 17.5 %copy.89 = f32[2,96,2,6,2,512]{5,4,2,3,1,0:T(2,128)} copy(f32[2,96,2,6,2,512]{5,2,1,4,3,0:T(2,128)} %reshape.171) | data formatting | bytes 18874368 | tf_op jit(solution)/shard_map/convert_element_type | solution.py:98
  471.7 16.9 %multiply_reduce_fusion = f32[2,96,6]{2,1,0:T(8,128)S(1)} fusion(f32[2,96,6]{2,1,0:T(8,128)S(1)} %broadcast_multiply_fusion.1, f32[2,96,2,6,2,512]{5,2,1,4,3,0:T(2,128)S(1)} %bitcast.95), kind=kLoop, calls=%fused_computation.25 | loop fusion | flops 7076736 | bytes 9446400 | tf_op jit(solution)/shard_map/reduce_sum | solution.py:19
  488.9 13.3 %reshape.167 = f32[1152,2048]{1,0:T(8,128)} reshape(f32[2,96,6,2,2,512]{5,4,3,2,1,0:T(2,128)} %bitcast.97) | data formatting | bytes 18874368 | tf_op jit(solution)/shard_map/convert_element_type | solution.py:98
  502.3 10.2 %fusion.22 = bf16[1152,1024]{1,0:T(8,128)(2,1)} fusion(bf16[2048,1024]{1,0:T(8,128)(2,1)} %param.11, f32[1152,2048]{1,0:T(8,128)} %reshape.167, f32[1152]{0:T(1024)S(1)} %rsqrt.25, f32[1152]{0:T(1024)S(1)} %div.28), kind=kOutput, calls=%fused_computation.42 | convolution fusion | flops 4840095744 | bytes 16000000 | tf_op jit(solution)/shard_map/dot_general | solution.py:99
  523.2 34.3 %all_to_all.18 = bf16[2,96,6,1024]{3,0,2,1:T(2,128)(2,1)S(1)} all-to-all(bf16[2,96,6,1024]{3,0,2,1:T(2,128)(2,1)S(1)} %copy.65), channel_id=1, replica_groups=mesh['lat'=4,'lon'=32] {'lon'}, dimensions={1} | all-to-all | bytes 4718592 | tf_op jit(solution)/shard_map/all_to_all | solution.py:105
  (80 shorter events, 110.5 us)
Async XLA Ops:
  0.0 141.4 %copy-start = (bf16[512,1536]{1,0:T(8,128)(2,1)S(1)}, bf16[512,1536]{1,0:T(8,128)(2,1)}, u32[]{:S(2)}) copy-start(bf16[512,1536]{1,0:T(8,128)(2,1)} %param.9) | copy-start | bytes 4718596
  1.1 7.9 %collective-permute-start = (bf16[2,3,12,512]{3,1,2,0:T(4,128)(2,1)S(1)}, bf16[2,3,12,512]{3,1,2,0:T(4,128)(2,1)S(1)}, u32[]{:S(2)}, u32[]{:S(2)}) collective-permute-start(bf16[2,3,12,512]{3,1,2,0:T(4,128)(2,1)S(1)} %slice.46), channel_id=1, source_target_pairs={{0,96},{32,0},{64,32},{96,64},{1,97},{33,1},{65,33},{97,65},{2,98}... | collective-permute-start | bytes 221192 | tf_op jit(solution)/shard_map/ppermute | solution.py:14
  9.0 9.3 %copy-start.4 = (s32[2,192,12]{1,0,2:T(2,128)S(1)}, s32[2,192,12]{1,0,2:T(2,128)}, u32[]{:S(2)}) copy-start(s32[2,192,12]{1,0,2:T(2,128)} %param.8) | copy-start | bytes 55300
  11.8 61.0 %collective-permute-start.1 = (bf16[2,192,6,512]{3,1,2,0:T(8,128)(2,1)}, bf16[2,192,6,512]{3,1,2,0:T(8,128)(2,1)}, u32[]{:S(2)}, u32[]{:S(2)}) collective-permute-start(bf16[2,192,6,512]{3,1,2,0:T(8,128)(2,1)} %get-tuple-element.55), channel_id=1, source_target_pairs={{0,31},{1,0},{2,1},{3,2},{4,3},{5,4},{6,5},{7,6},{8,7},{9,8},{10,9... | collective-permute-start | bytes 7077896 | tf_op jit(solution)/shard_map/ppermute | solution.py:14
  18.3 49.9 %collective-permute-start.2 = (bf16[2,3,12]{1,0,2:T(2,128)(2,1)S(1)}, bf16[2,3,12]{1,0,2:T(2,128)(2,1)S(1)}, u32[]{:S(2)}, u32[]{:S(2)}) collective-permute-start(bf16[2,3,12]{1,0,2:T(2,128)(2,1)S(1)} %slice.63), channel_id=1, source_target_pairs={{0,96},{32,0},{64,32},{96,64},{1,97},{33,1},{65,33},{97,65},{2,98}... | collective-permute-start | bytes 440 | tf_op jit(solution)/shard_map/ppermute | solution.py:14
  68.3 3.7 collective-permute-start.3
  115.2 10.7 %copy-start.2 = (f32[32,2,6,12]{1,3,2,0:T(8,128)S(1)}, f32[32,2,6,12]{1,3,2,0:T(8,128)}, u32[]{:S(2)}) copy-start(f32[32,2,6,12]{1,3,2,0:T(8,128)} %multiply_reduce_fusion.1) | copy-start | bytes 55300
  359.5 64.4 %slice-start.3 = ((s8[4718592]{0:T(1024)(128)(4,1)}), s8[4194304]{0:T(1024)(128)(4,1)S(1)}, s32[]{:S(2)}) async-start(s8[4718592]{0:T(1024)(128)(4,1)} %bitcast.98), calls=%async_computation.4 | async-start | bytes 8388608
  360.0 63.9 %slice-start.4 = ((s8[4718592]{0:T(1024)(128)(4,1)}), s8[524288]{0:T(1024)(128)(4,1)S(1)}, s32[]{:S(2)}) async-start(s8[4718592]{0:T(1024)(128)(4,1)} %bitcast.98), calls=%async_computation.5 | async-start | bytes 1048576
  360.0 63.9 %copy-start.3 = (bf16[512,512]{1,0:T(8,128)(2,1)S(1)}, bf16[512,512]{1,0:T(8,128)(2,1)}, u32[]{:S(2)}) copy-start(bf16[512,512]{1,0:T(8,128)(2,1)} %param.10) | copy-start | bytes 1572868
  360.1 57.6 %collective-permute-start.4 = (bf16[2,192,6,512]{3,1,2,0:T(8,128)(2,1)S(1)}, bf16[2,192,6,512]{3,1,2,0:T(8,128)(2,1)S(1)}, u32[]{:S(2)}, u32[]{:S(2)}) collective-permute-start(bf16[2,192,6,512]{3,1,2,0:T(8,128)(2,1)S(1)} %copy.75), channel_id=1, source_target_pairs={{0,1},{1,2},{2,3},{3,4},{4,5},{5,6},{6,7},{7,8},{8,9},{9,10},{10,1... | collective-permute-start | bytes 7077896 | tf_op jit(solution)/shard_map/ppermute | solution.py:14
  418.4 5.6 collective-permute-start.5
  442.1 29.6 %slice-start = ((s8[9437184]{0:T(1024)(128)(4,1)}), s8[1048576]{0:T(1024)(128)(4,1)S(1)}, s32[]{:S(2)}) async-start(s8[9437184]{0:T(1024)(128)(4,1)} %bitcast.94), calls=%async_computation.1 | async-start | bytes 2097152
  454.1 17.6 %slice-start.1 = ((s8[9437184]{0:T(1024)(128)(4,1)}), s8[4194304]{0:T(1024)(128)(4,1)S(1)}, s32[]{:S(2)}) async-start(s8[9437184]{0:T(1024)(128)(4,1)} %bitcast.94), calls=%async_computation.2 | async-start | bytes 8388608
  454.1 17.6 %slice-start.2 = ((s8[9437184]{0:T(1024)(128)(4,1)}), s8[4194304]{0:T(1024)(128)(4,1)S(1)}, s32[]{:S(2)}) async-start(s8[9437184]{0:T(1024)(128)(4,1)} %bitcast.94), calls=%async_computation.3 | async-start | bytes 8388608
  557.5 3.9 copy-start.1
where the time goes:
time: 570 us; the launch traced here: 562 us
  local copies, waits for them, and re-layouts  240 us (42%)
  waiting for transfers between devices  114 us (20%)
  matrix products  103 us (18%)
  other arithmetic  58.3 us (10%)
  blocking collectives  34.3 us (6%)
  starting transfers between devices  11.6 us (2%)
    ppermute x6, waiting for transfers between devices, shifted(): return lax.ppermute(value, axis, pairs)  114 us
    reshape x1, local copies, waits for them, and re-layouts, attend_tile(): packed.reshape(group_count, per_group, window_span, 3, HEADS, head_size)  44.4 us
    convert_element_type x3, local copies, waits for them, and re-layouts, body(): merge_in = normalize(grouped.astype(jnp.float32)).astype(jnp.bfloat16)  43.2 us
    sub x2, matrix products, one_group(): weights = jnp.exp(scores - peak_score)  39.8 us
    convert_element_type x3, local copies, waits for them, and re-layouts, attend_tile(): normed = normalize(ordered.astype(jnp.float32)).astype(jnp.bfloat16)  37.8 us
    all_to_all x1, blocking collectives, body(): lax.all_to_all(merged, 'lon', split_axis=1, concat_axis=2, tiled=True)  34.3 us
    dot_general x2, matrix products, one_group(): jnp.einsum('whqk,wkhd->wqhd', weights, values_in, preferred_element_type=...  33 us
    dynamic_slice x4, local copies, waits for them, and re-layouts, attend_tile(): mixed_out = lax.map(one_group, (packed, window_labels))  31.8 us
  transfers between devices with their start and end apart: 6, of which 4 were waited for; matrix products, arithmetic and copies ran while one was open for 1% of the time, Pallas kernels for 0%

commit v1 on v0

v1 whole, which is shorter than its diff:
```python
import functools

import jax
import jax.numpy as jnp
import numpy as np
from jax import lax
from jax.experimental import pallas as pl
from jax.experimental.pallas import tpu as pltpu
from jax.sharding import PartitionSpec as P

MESH = pl.DeviceIdType.MESH
HEADS = 16
WIN_LAT = 6
WIN_LON = 12
LEV = 2
HALF = 72
SPAN = 144
PADDED = 160
GROUP = 4
F32 = jnp.float32
BF16 = jnp.bfloat16


def tables():
    pick_own = np.zeros((HALF, 192), np.float32)
    pick_west = np.zeros((HALF, 192), np.float32)
    order = np.zeros((PADDED, SPAN), np.float32)
    pack = np.zeros((SPAN, PADDED), np.float32)
    for lev in range(LEV):
        for row in range(6):
            for col in range(6):
                place = (lev * 6 + row) * 6 + col
                pick_own[place, (lev * 6 + row) * 16 + col + 6] = 1
                pick_west[place, (lev * 6 + row) * 16 + col] = 1
    window_rows = ((5, 1, 3), (0, 2, 4))
    for odd in range(2):
        for right in range(2):
            block = odd * 2 + right
            for slot in range(3):
                for lev in range(LEV):
                    for patch in range(6):
                        half, col = divmod(patch, 3)
                        token = half * HALF + (lev * 6 + window_rows[odd][slot]) * 6 + 2 * col + right
                        order[block * 40 + slot * 12 + lev * 6 + patch, token] = 1
    for slot in range(3):
        for lanes in range(4):
            for place in range(12):
                pack[slot * 48 + lanes * 12 + place, lanes * 40 + slot * 12 + place] = 1
    return [jnp.asarray(t, BF16) for t in (pick_own, pick_west, order, pack)]


def dot(a, b):
    return jnp.dot(a, b, preferred_element_type=F32)


def dot_nt(a, b):
    return lax.dot_general(a, b, (((1,), (1,)), ((), ())), preferred_element_type=F32)


def normalize(values):
    center = values - jnp.mean(values, -1, keepdims=True)
    spread = jnp.mean(center * center, -1, keepdims=True)
    return center * lax.rsqrt(spread + 1e-05)


def raw_window(tok, window):
    raw = tok[:, pl.ds(6 * window + 3, 6)]
    return jnp.pad(raw, ((0, 0), (0, 0), (0, 4), (0, 0))).reshape(192, raw.shape[-1])


def fused(
    n_lat,
    n_lon,
    tokens,
    labels,
    pick_own,
    pick_west,
    order,
    pack,
    w_qk_hbm,
    w_vt_hbm,
    w_out_hbm,
    w_merge_hbm,
    recv,
    tok,
    halo,
    west,
    stage,
    w_qk,
    w_vt,
    w_out,
    w_merge,
    xs,
    ns,
    qs,
    ks,
    wos,
    carry,
    odd_save,
    carry_send,
    carry_recv,
    load_sems,
    row_sems,
    halo_send,
    halo_recv,
    carry_sems,
    out_send,
    out_recv,
):
    lat = lax.axis_index("lat")
    lon = lax.axis_index("lon")
    next_lat = lax.rem(lat + 1, n_lat)
    prev_lat = lax.rem(lat + n_lat - 1, n_lat)
    west_lon = lax.rem(lon + n_lon - 1, n_lon)
    rows = tokens.shape[1]
    windows = rows // WIN_LAT
    chunks = windows // GROUP
    span_rows = GROUP * HALF
    first = lax.rem((lon * chunks) // n_lon, chunks)
    first_west = lax.rem((west_lon * chunks) // n_lon, chunks)

    loads = [
        pltpu.make_async_copy(tokens, tok.at[:, pl.ds(0, rows)], load_sems.at[0]),
        pltpu.make_async_copy(w_qk_hbm, w_qk, load_sems.at[1]),
        pltpu.make_async_copy(w_vt_hbm, w_vt, load_sems.at[2]),
        pltpu.make_async_copy(w_out_hbm, w_out, load_sems.at[3]),
        pltpu.make_async_copy(w_merge_hbm, w_merge, load_sems.at[4]),
    ]
    for load in loads:
        load.start()

    barrier = pltpu.get_barrier_semaphore()

    def greet(step, _):
        other = lax.rem(lon + step, n_lon)
        pl.semaphore_signal(barrier, inc=1, device_id=(lat, other), device_id_type=MESH)
        return 0

    lax.fori_loop(1, n_lon, greet, 0)
    pl.semaphore_signal(barrier, inc=1, device_id=(prev_lat, lon), device_id_type=MESH)
    pl.semaphore_signal(barrier, inc=1, device_id=(next_lat, lon), device_id_type=MESH)

    @pl.when(lon == 0)
    def _():
        def greet_before(other, _):
            pl.semaphore_signal(barrier, inc=1, device_id=(prev_lat, other), device_id_type=MESH)
            return 0

        lax.fori_loop(0, n_lon, greet_before, 0)

    loads[0].wait()
    pl.semaphore_wait(barrier, n_lon + 2)

    rows_copy = pltpu.make_async_remote_copy(
        src_ref=tok.at[:, pl.ds(0, 3)],
        dst_ref=tok.at[:, pl.ds(rows, 3)],
        send_sem=row_sems.at[0],
        recv_sem=row_sems.at[1],
        device_id=(prev_lat, lon),
        device_id_type=MESH,
    )
    rows_copy.start()

    def halo_copy(chunk):
        return pltpu.make_async_remote_copy(
            src_ref=west.at[chunk],
            dst_ref=halo.at[chunk],
            send_sem=halo_send.at[chunk],
            recv_sem=halo_recv.at[chunk],
            device_id=(lat, west_lon),
            device_id_type=MESH,
        )

    def send_west(step, _):
        chunk = lax.rem(first_west + step, chunks)

        @pl.when(chunk == chunks - 1)
        def _():
            rows_copy.wait_recv()

        parts = [
            dot(pick_west[...], raw_window(tok, chunk * GROUP + i)) for i in range(GROUP)
        ]
        west[chunk] = jnp.concatenate(parts, 0).astype(BF16)
        halo_copy(chunk).start()
        return 0

    lax.fori_loop(0, chunks, send_west, 0)
    rows_copy.wait_send()
    for load in loads[1:]:
        load.wait()

    score_scale = 32 ** (-0.5) * 1.4426950408889634
    head_of_lane = lax.broadcasted_iota(jnp.int32, (SPAN, 128), 1) // 32
    head_of_row = lax.broadcasted_iota(jnp.int32, (128, 128), 0) // 32
    tail_head = lax.broadcasted_iota(jnp.int32, (128, 64), 1) // 16
    tail_row = lax.broadcasted_iota(jnp.int32, (128, 64), 0) // 32
    sum_row = lax.broadcasted_iota(jnp.int32, (16, 512), 0)
    sum_lane = lax.broadcasted_iota(jnp.int32, (16, 512), 1) // 128
    tail_sum_row = lax.broadcasted_iota(jnp.int32, (16, 64), 0)
    tail_sum_lane = lax.broadcasted_iota(jnp.int32, (16, 64), 1) // 16
    sum_rows = jnp.concatenate(
        [(sum_row == sum_lane).astype(F32), (tail_sum_row == tail_sum_lane).astype(F32)], 1
    ).astype(BF16)
    label_rows = lax.broadcasted_iota(jnp.int32, (128, SPAN), 0).astype(F32)
    eye_row = lax.broadcasted_iota(jnp.int32, (SPAN, SPAN), 0)
    eye = (eye_row == lax.broadcasted_iota(jnp.int32, (SPAN, SPAN), 1)).astype(F32).astype(BF16)

    def stacked(value):
        return jnp.concatenate([value[:128]] * 4 + [value[128:]] * 4, 0)

    def attend_window(window, i):
        base = pl.multiple_of(i * SPAN, 16)
        normed = ns[pl.ds(base, SPAN)]
        value_t = dot_nt(
            w_vt[...], jnp.concatenate([normed[:128]] + [normed[128:]] * 4, 0)
        ).astype(BF16)
        lane_labels = labels[pl.ds(window, 1), :SPAN]
        marks_t = (label_rows == lane_labels).astype(F32).astype(BF16)
        marks = dot_nt(eye, marks_t)
        query_marks = marks.astype(BF16)
        key_marks = stacked(((marks - 1.0) * 1e30).astype(BF16))
        outs = []
        for g in range(HEADS // 4):
            lanes = pl.ds(g * 128, 128)
            query = jnp.concatenate([qs[pl.ds(base, SPAN), lanes], query_marks], 1)
            key = ks[pl.ds(base, SPAN), lanes]
            heads = [jnp.where(head_of_lane == h, key, jnp.zeros_like(key)) for h in range(4)]
            keys = jnp.concatenate([k[:128] for k in heads] + [k[128:] for k in heads], 0)
            keys = jnp.concatenate([keys, key_marks], 1)
            scores = dot_nt(keys, query)
            mains, tails = [], []
            for h in range(4):
                main = scores[128 * h : 128 * h + 128]
                tail = scores[512 + 16 * h : 528 + 16 * h]
                peak = jnp.maximum(
                    jnp.max(main, 0, keepdims=True), jnp.max(tail, 0, keepdims=True)
                )
                mains.append(jnp.exp2((main - peak).astype(BF16)))
                tails.append(jnp.exp2((tail - peak).astype(BF16)))
            weights = jnp.concatenate(mains + tails, 0)
            group_values = value_t[g * 128 : g * 128 + 128]
            main_values = group_values[:, :128]
            tail_values = group_values[:, 128:192]
            parts = [
                jnp.where(head_of_row == h, main_values, jnp.zeros_like(main_values))
                for h in range(4)
            ]
            parts.append(jnp.where(tail_head == tail_row, tail_values, jnp.zeros_like(tail_values)))
            values = jnp.concatenate([jnp.concatenate(parts, 1), sum_rows], 0)
            result = dot(values, weights)
            scale = 1.0 / result[128:136]
            for h in range(4):
                outs.append(result[32 * h : 32 * h + 32] * scale[h : h + 1])
        out_t = jnp.concatenate(outs, 0).astype(BF16)
        wos[pl.ds(pl.multiple_of(i * PADDED, 16), PADDED)] = dot_nt(order[...], out_t).astype(BF16)
        return 0

    def merge(blocks):
        total = sum(jnp.sum(b, -1, keepdims=True) for b in blocks)
        mean = total * (1.0 / 2048)
        blocks = [b - mean for b in blocks]
        spread = sum(jnp.sum(b * b, -1, keepdims=True) for b in blocks) * (1.0 / 2048)
        factor = lax.rsqrt(spread + 1e-05)
        merge_in = jnp.concatenate([(b * factor).astype(BF16) for b in blocks], 1)
        return dot(merge_in, w_merge[...])

    def packed(rows40):
        stacked_lanes = jnp.concatenate([rows40[:, 256 * j : 256 * j + 256] for j in range(4)], 0)
        return dot(pack[...], stacked_lanes.astype(BF16)).astype(BF16)

    def own_copy():
        return pltpu.make_async_copy(
            stage.at[pl.ds(3 * lon, 3)], recv.at[lon], out_recv
        )

    def send_copy(owner):
        return pltpu.make_async_remote_copy(
            src_ref=stage.at[pl.ds(3 * owner, 3)],
            dst_ref=recv.at[lon],
            send_sem=out_send.at[owner],
            recv_sem=out_recv,
            device_id=(lat, owner),
            device_id_type=MESH,
        )

    def own_zero_copy():
        return pltpu.make_async_copy(
            stage.at[pl.ds(1, 2)], recv.at[lon, pl.ds(1, 2)], out_recv
        )

    def send_zero_copy():
        return pltpu.make_async_remote_copy(
            src_ref=stage.at[pl.ds(1, 2)],
            dst_ref=recv.at[lon, pl.ds(1, 2)],
            send_sem=out_send.at[0],
            recv_sem=out_recv,
            device_id=(lat, 0),
            device_id_type=MESH,
        )

    def last_copy():
        return pltpu.make_async_remote_copy(
            src_ref=stage.at[pl.ds(3 * windows, 1)],
            dst_ref=recv.at[lon, pl.ds(0, 1)],
            send_sem=out_send.at[windows],
            recv_sem=out_recv,
            device_id=(next_lat, 0),
            device_id_type=MESH,
        )

    def send(owner):
        @pl.when(owner == lon)
        def _():
            own_copy().start()

        @pl.when(owner != lon)
        def _():
            send_copy(owner).start()

    carry_copy = pltpu.make_async_remote_copy(
        src_ref=carry_send,
        dst_ref=carry_recv,
        send_sem=carry_sems.at[0],
        recv_sem=carry_sems.at[1],
        device_id=(next_lat, lon),
        device_id_type=MESH,
    )

    carry[...] = jnp.zeros_like(carry)
    slot_row = lax.broadcasted_iota(jnp.int32, (GROUP * 40, 512), 0) % 40 < 12

    def chunk_step(step, _):
        chunk = lax.rem(first + step, chunks)
        start = chunk * GROUP

        @pl.when(chunk == chunks - 1)
        def _():
            @pl.when(first_west != chunks - 1)
            def _():
                pass

        halo_copy(chunk).wait_recv()
        for i in range(GROUP):
            own = dot(pick_own[...], raw_window(tok, start + i))
            east = halo[chunk, pl.ds(i * HALF, HALF)].astype(F32) if (i * HALF) % 16 == 0 else None
            if east is None:
                east = halo[chunk, pl.ds(i * HALF - 8, HALF + 8)].astype(F32)[8:]
            value = jnp.concatenate([own, east], 0)
            xs[pl.ds(i * SPAN, SPAN)] = value.astype(BF16)
            ns[pl.ds(i * SPAN, SPAN)] = normalize(value).astype(BF16)
        qs[...] = (dot(ns[...], w_qk[:, :512]) * score_scale).astype(BF16)
        ks[...] = dot(ns[...], w_qk[:, 512:]).astype(BF16)
        lax.fori_loop(0, GROUP, lambda i, _: attend_window(start + i, i), 0)
        residual = jnp.concatenate(
            [dot(order[...], xs[pl.ds(i * SPAN, SPAN)]) for i in range(GROUP)], 0
        )
        updated = (residual + dot(wos[...], w_out[...])).astype(BF16).astype(F32)
        blocks = []
        for p in range(4):
            pieces = [
                updated[PADDED * i + 40 * p : PADDED * i + 40 * p + 40] for i in range(GROUP)
            ]
            block = jnp.concatenate(pieces, 0)
            if p < 2:
                before = jnp.concatenate([carry[pl.ds(40 * p, 40)]] + pieces[:-1], 0)
                carry[pl.ds(40 * p, 40)] = pieces[-1]
                block = jnp.where(slot_row, before, block)
            blocks.append(block)

        @pl.when(step == 0)
        def _():
            for p in range(2):
                odd_save[1, pl.ds(16 * p, 16)] = blocks[2 + p][:16]

        @pl.when(chunk == 0)
        def _():
            for p in range(2):
                odd_save[0, pl.ds(16 * p, 16)] = blocks[2 + p][:16]

        @pl.when(chunk == chunks - 1)
        def _():
            for p in range(2):
                carry_send[pl.ds(16 * p, 16)] = carry[pl.ds(40 * p, 16)].astype(BF16)
            carry_copy.start()

        merged = merge(blocks)
        for i in range(GROUP):
            pieces = packed(merged[40 * i : 40 * i + 40])
            for slot in range(3):
                if i == 0 and slot == 0:
                    stage[3 * start + 1] = pieces[:48]
                else:
                    stage[3 * (start + i) + 1 + slot] = pieces[48 * slot : 48 * slot + 48]
            owner = start + i
            if i == 0:

                @pl.when(jnp.logical_and(step > 0, chunk > 0))
                def _():
                    send(owner)
            else:
                send(owner)

        @pl.when(chunk == chunks - 1)
        def _():
            last_copy().start()

        return 0

    lax.fori_loop(0, chunks, chunk_step, 0)

    carry_copy.wait_recv()
    lat_carry = carry_recv[...].astype(F32)
    blocks = []
    for p in range(2):
        blocks.append(
            jnp.concatenate([lat_carry[16 * p : 16 * p + 16], carry[pl.ds(40 * p, 16)]], 0)
        )
    for p in range(2):
        blocks.append(
            jnp.concatenate([odd_save[0, pl.ds(16 * p, 16)], odd_save[1, pl.ds(16 * p, 16)]], 0)
        )
    merged = merge(blocks)
    zero_rows = jnp.zeros((24, merged.shape[1]), F32)
    stage[1] = packed(jnp.concatenate([merged[:16], zero_rows], 0))[:48]

    @pl.when(lon == 0)
    def _():
        own_zero_copy().start()

    @pl.when(lon != 0)
    def _():
        send_zero_copy().start()

    @pl.when(first != 0)
    def _():
        stage[3 * GROUP * first + 1] = packed(jnp.concatenate([merged[16:], zero_rows], 0))[:48]
        send(GROUP * first)

    def wait_halo(chunk, _):
        halo_copy(chunk).wait_send()
        return 0

    lax.fori_loop(0, chunks, wait_halo, 0)
    carry_copy.wait_send()
    last_copy().wait_send()

    @pl.when(lon != 0)
    def _():
        send_zero_copy().wait_send()

    def wait_send(owner, _):
        @pl.when(owner != lon)
        def _():
            send_copy(owner).wait_send()

        return 0

    lax.fori_loop(1, windows, wait_send, 0)
    pltpu.make_async_copy(recv, recv, out_recv).wait()


def exchange(tokens, labels, w_qkv, w_out, w_merge, n_lat, n_lon):
    levels, rows, cols, channels = tokens.shape
    windows = rows // WIN_LAT
    chunks = windows // GROUP
    vmem = pl.BlockSpec(memory_space=pltpu.VMEM)
    hbm = pl.BlockSpec(memory_space=pl.ANY)
    w_qk = w_qkv[:, : 2 * channels]
    w_vt = w_qkv[:, 2 * channels :].T
    span = GROUP * SPAN
    return pl.pallas_call(
        functools.partial(fused, n_lat, n_lon),
        out_shape=jax.ShapeDtypeStruct((n_lon, 3, 48, 256), BF16),
        in_specs=[hbm] + [vmem] * 5 + [hbm] * 4,
        out_specs=hbm,
        scratch_shapes=[
            pltpu.VMEM((levels, rows + 3, cols, channels), BF16),
            pltpu.VMEM((chunks, GROUP * HALF, channels), BF16),
            pltpu.VMEM((chunks, GROUP * HALF, channels), BF16),
            pltpu.VMEM((3 * windows + 1, 48, 256), BF16),
            pltpu.VMEM((channels, 2 * channels), BF16),
            pltpu.VMEM((channels, channels), BF16),
            pltpu.VMEM((channels, channels), BF16),
            pltpu.VMEM((4 * channels, 2 * channels), BF16),
            pltpu.VMEM((span, channels), BF16),
            pltpu.VMEM((span, channels), BF16),
            pltpu.VMEM((span, channels), BF16),
            pltpu.VMEM((span, channels), BF16),
            pltpu.VMEM((GROUP * PADDED, channels), BF16),
            pltpu.VMEM((80, channels), F32),
            pltpu.VMEM((2, 32, channels), F32),
            pltpu.VMEM((32, channels), BF16),
            pltpu.VMEM((32, channels), BF16),
            pltpu.SemaphoreType.DMA((5,)),
            pltpu.SemaphoreType.DMA((2,)),
            pltpu.SemaphoreType.DMA((chunks,)),
            pltpu.SemaphoreType.DMA((chunks,)),
            pltpu.SemaphoreType.DMA((2,)),
            pltpu.SemaphoreType.DMA((windows + 1,)),
            pltpu.SemaphoreType.DMA,
        ],
        compiler_params=pltpu.CompilerParams(
            collective_id=0, has_side_effects=True, vmem_limit_bytes=56 * 1024 * 1024
        ),
        name="attend_merge_send",
    )(tokens, labels, *tables(), w_qk, w_vt, w_out, w_merge)


def shifted(value, axis, steps):
    count = lax.axis_size(axis)
    pairs = [(source, (source + steps) % count) for source in range(count)]
    return lax.ppermute(value, axis, pairs)


def window_labels(region, n_lat):
    levels, rows, cols = region.shape
    windows = rows // WIN_LAT
    marks = (region * 2).astype(F32)
    after = shifted(marks[:, :3], "lat", -1)
    after = after + (lax.axis_index("lat") == n_lat - 1).astype(F32)
    marks = jnp.concatenate([marks[:, 3:], after], 1)
    halves = marks.reshape(levels, windows, WIN_LAT, 2, WIN_LON // 2)
    halves = halves.transpose(3, 1, 0, 2, 4).reshape(2, windows, HALF)
    east = shifted(halves[0], "lon", -1)
    return jnp.concatenate([halves[1], east, jnp.full((windows, 256 - SPAN), 9.0, F32)], 1)


def arrange(recv, n_lon):
    parts = recv.reshape(n_lon, 3, 4, LEV, 2, 3, 256)
    own, east = parts[..., 0, :, :], parts[..., 1, :, :]
    east = jnp.roll(east, 1, 0)
    parts = jnp.stack([east, own], 4)
    parts = parts.transpose(3, 1, 0, 4, 5, 2, 6)
    return parts.reshape(LEV, 3, n_lon * 6, 1024)


def solution(mesh):
    n_lat, n_lon = mesh.shape["lat"], mesh.shape["lon"]

    def body(tokens, region, w_qkv, w_out, w_merge):
        labels = window_labels(region, n_lat)
        recv = exchange(tokens, labels, w_qkv, w_out, w_merge, n_lat, n_lon)
        return arrange(recv, n_lon)

    in_specs = (P(None, "lat", "lon", None), P(None, "lat", "lon"), P(), P(), P())
    out_specs = P(None, ("lat", "lon"), None, None)
    return jax.shard_map(body, mesh=mesh, in_specs=in_specs, out_specs=out_specs, check_vma=False)
```

time: 570 us -> 157 us (0.28); the launches traced: 562 us -> 156 us
  local copies, waits for them, and re-layouts: 240 us -> 18.7 us
  Pallas kernels: 0 us -> 124 us
  waiting for transfers between devices: 114 us -> 1.31 us
  matrix products: 103 us -> 0 us
  other arithmetic: 58.3 us -> 2.53 us
  blocking collectives: 34.3 us -> 0 us
    pallas_call x0 -> x1, Pallas kernels: none -> 124 us  [exchange(): pl.pallas_call(functools.partial(fused, n_lat, n_lon), out_shape=jax.Shap...]
    ppermute x6 -> x2, waiting for transfers between devices: 114 us -> 1.31 us  [shifted(): return lax.ppermute(value, axis, pairs)]
    convert_element_type x7 -> x0, local copies, waits for them, and re-layouts: 99.8 us -> none  [the longest x3 43.2 us: body(): merge_in = normalize(grouped.astype(jnp.float32)).astype(jnp.bfloat16)]
    dot_general x5 -> x0, matrix products: 62.9 us -> none  [the longest x2 33 us: one_group(): jnp.einsum('whqk,wkhd->wqhd', weights, values_in, preferred_element_type=...]
    reshape x3 -> x2, local copies, waits for them, and re-layouts: 55.2 us -> 3.27 us  [the longest x1 2.89 us: arrange(): return parts.reshape(LEV, 3, n_lon * 6, 1024)]
    reduce_sum x4 -> x0, other arithmetic: 49.9 us -> none  [the longest x2 28.5 us: normalize(): spread = jnp.mean(center * center, -1, keepdims=True)]
    sub x2 -> x0, matrix products: 39.8 us -> none  [one_group(): weights = jnp.exp(scores - peak_score)]
    all_to_all x1 -> x0, blocking collectives: 34.3 us -> none  [body(): lax.all_to_all(merged, 'lon', split_axis=1, concat_axis=2, tiled=True)]
  transfers between devices with their start and end apart: 6 -> 2, of which waited for: 4 -> 1; matrix products, arithmetic and copies ran while one was open for 1% -> 7% of each run, Pallas kernels for 0% -> 0%
where the time goes in v1:
time: 157 us; the launch traced here: 156 us
  Pallas kernels  124 us (79%)
  local copies, waits for them, and re-layouts  18.7 us (12%)
  starting transfers between devices  9.15 us (6%)
  other arithmetic  2.53 us (2%)
    pallas_call x1, Pallas kernels, exchange(): pl.pallas_call(functools.partial(fused, n_lat, n_lon), out_shape=jax.Shap...  124 us
    ppermute x2, starting transfers between devices, shifted(): return lax.ppermute(value, axis, pairs)  9.15 us
    unnamed x4, local copies, waits for them, and re-layouts  8.93 us
  transfers between devices with their start and end apart: 2, of which 1 were waited for; matrix products, arithmetic and copies ran while one was open for 7% of the time, Pallas kernels for 0%

profile of v1, /device:TPU:0, one launch (start us, length us, event | category | flops | bytes accessed | tf_op | source)
XLA Modules:
  0.0 155.7 jit_solution(519479803349308447)
XLA Ops:
  0.0 0.9 multiply_convert_fusion
  0.9 2.6 %collective-permute-start = (f32[2,3,12]{1,0,2:T(2,128)S(1)}, f32[2,3,12]{1,0,2:T(2,128)S(1)}, u32[]{:S(2)}, u32[]{:S(2)}) collective-permute-start(f32[2,3,12]{1,0,2:T(2,128)S(1)} %slice.52), channel_id=1, source_target_pairs={{0,96},{32,0},{64,32},{96,64},{1,97},{33,1},{65,33},{97,65},{2,98}... | collective-permute-start | bytes 872 | tf_op jit(solution)/shard_map/ppermute | solution.py:513
  3.5 0.1 slice.51
  3.6 1.3 collective-permute-done
  4.9 0.1 pad_maximum_fusion
  5.0 0.4 reshape.16
  5.4 0.2 copy.26
  5.7 6.5 %collective-permute-start.1 = (f32[32,72]{1,0:T(8,128)S(1)}, f32[32,72]{1,0:T(8,128)S(1)}, u32[]{:S(2)}, u32[]{:S(2)}) collective-permute-start(f32[32,72]{1,0:T(8,128)S(1)} %copy.27), channel_id=1, source_target_pairs={{0,31},{1,0},{2,1},{3,2},{4,3},{5,4},{6,5},{7,6},{8,7},{9,8},{10,9... | collective-permute-start | bytes 27656 | tf_op jit(solution)/shard_map/ppermute | solution.py:513
  12.2 1.1 slice.44.w_qk_hbm
  13.4 1.1 copy.36
  14.4 7.9 %copy.30.tokens = bf16[2,192,12,512]{3,2,1,0:T(8,128)(2,1)} copy(bf16[2,192,12,512]{3,1,2,0:T(8,128)(2,1)} %param.9) | data formatting | bytes 9437184 | tf_op args[0]
  22.3 0.1 pad.6.clone
  22.4 0.2 copy.25
  22.5 0.1 copy.28
  22.6 0.7 maximum_maximum_fusion.labels
  23.3 123.8 %attend_merge_send.1 = bf16[32,3,48,256]{3,2,1,0:T(8,128)(2,1)} custom-call(bf16[2,192,12,512]{3,2,1,0:T(8,128)(2,1)} %copy.30.tokens, f32[32,256]{1,0:T(8,128)} %maximum_maximum_fusion.labels, bf16[72,192]{1,0:T(8,128)(2,1)} %constant.20.clone.pick_own, bf16[72,192]{1,0:T(8,128)(2,1)} %constant.21.clone.pick_west, bf16[160,144]{1,0:T(8,128)(2,1)} %constant.22.clone.order, ...), custom_call_target="tpu_custom_call" | custom-call | tf_op jit(solution)/shard_map/attend_merge_send/pallas_call | solution.py:472
  147.2 2.5 %copy.31 = bf16[32,3,48,256]{3,0,2,1:T(8,128)(2,1)S(1)} copy(bf16[32,3,48,256]{3,2,1,0:T(8,128)(2,1)} %attend_merge_send.1) | data formatting | bytes 4718592 | tf_op jit(solution)/shard_map/attend_merge_send/pallas_call | solution.py:472
  149.7 0.1 slice.55
  149.8 0.1 slice.57
  149.9 0.1 slice_bitcast_fusion
  150.1 0.6 maximum_bitcast_fusion.1
  150.8 0.2 maximum_bitcast_fusion
  151.0 1.8 %copy.35 = bf16[2,3,32,2,3,4,256]{6,5,4,3,2,1,0:T(4,128)(2,1)S(1)} copy(bf16[2,3,32,2,3,4,256]{6,2,4,3,0,5,1:T(8,128)(2,1)S(1)} %maximum_bitcast_fusion) | data formatting | bytes 4718592 | tf_op jit(solution)/shard_map/transpose | solution.py:534
  152.8 2.9 %reshape.18 = bf16[2,3,192,1024]{3,2,1,0:T(8,128)(2,1)} reshape(bf16[2,3,32,2,3,4,256]{6,5,4,3,2,1,0:T(4,128)(2,1)S(1)} %copy.35) | data formatting | bytes 4718592 | tf_op jit(solution)/shard_map/reshape | solution.py:535
  (14 shorter events, 0.2 us)
Async XLA Ops:
  0.0 12.2 %copy-start = (bf16[512,1536]{1,0:T(8,128)(2,1)S(1)}, bf16[512,1536]{1,0:T(8,128)(2,1)}, u32[]{:S(2)}) copy-start(bf16[512,1536]{1,0:T(8,128)(2,1)} %param.11) | copy-start | bytes 4718596
  0.9 4.0 %collective-permute-start = (f32[2,3,12]{1,0,2:T(2,128)S(1)}, f32[2,3,12]{1,0,2:T(2,128)S(1)}, u32[]{:S(2)}, u32[]{:S(2)}) collective-permute-start(f32[2,3,12]{1,0,2:T(2,128)S(1)} %slice.52), channel_id=1, source_target_pairs={{0,96},{32,0},{64,32},{96,64},{1,97},{33,1},{65,33},{97,65},{2,98}... | collective-permute-start | bytes 872 | tf_op jit(solution)/shard_map/ppermute | solution.py:513
  5.0 8.4 %slice-start = ((bf16[512,1536]{1,0:T(8,128)(2,1)}), bf16[512,512]{1,0:T(8,128)(2,1)S(1)}, s32[]{:S(2)}) async-start(bf16[512,1536]{1,0:T(8,128)(2,1)} %param.11), calls=%async_computation | async-start | bytes 1048576 | tf_op jit(solution)/shard_map/slice | solution.py:470
  5.7 16.9 %collective-permute-start.1 = (f32[32,72]{1,0:T(8,128)S(1)}, f32[32,72]{1,0:T(8,128)S(1)}, u32[]{:S(2)}, u32[]{:S(2)}) collective-permute-start(f32[32,72]{1,0:T(8,128)S(1)} %copy.27), channel_id=1, source_target_pairs={{0,31},{1,0},{2,1},{3,2},{4,3},{5,4},{6,5},{7,6},{8,7},{9,8},{10,9... | collective-permute-start | bytes 27656 | tf_op jit(solution)/shard_map/ppermute | solution.py:513

commit v2 on v1

v2 whole, which is shorter than its diff:
```python
import functools

import jax
import jax.numpy as jnp
import numpy as np
from jax import lax
from jax.experimental import pallas as pl
from jax.experimental.pallas import tpu as pltpu
from jax.sharding import PartitionSpec as P

MESH = pl.DeviceIdType.MESH
HEADS = 16
WIN_LAT = 6
WIN_LON = 12
LEV = 2
BLOCK = 192
SPAN = 144
PADDED = 160
GROUP = 4
PICK_STARTS = (0, 1, 1, 2)
PICK_ROWS = (3, 1, 7, 5)
F32 = jnp.float32
BF16 = jnp.bfloat16


def tables():
    pick = np.zeros((SPAN, 2 * BLOCK), np.float32)
    order = np.zeros((PADDED, SPAN), np.float32)
    pack = np.zeros((SPAN, PADDED), np.float32)
    picks = []
    for offset in PICK_ROWS:
        pick = np.zeros((SPAN, 2 * BLOCK), np.float32)
        for line in range(24):
            for row in range(6):
                pick[line * 6 + row, line * 16 + offset + row] = 1
        picks.append(pick)
    window_rows = ((5, 1, 3), (0, 2, 4))
    for odd in range(2):
        for right in range(2):
            block = odd * 2 + right
            for slot in range(3):
                for lev in range(LEV):
                    for patch in range(6):
                        half, col = divmod(patch, 3)
                        line = half * 12 + lev * 6 + 2 * col + right
                        token = line * 6 + window_rows[odd][slot]
                        order[block * 40 + slot * 12 + lev * 6 + patch, token] = 1
    for slot in range(3):
        for lanes in range(4):
            for place in range(12):
                pack[slot * 48 + lanes * 12 + place, lanes * 40 + slot * 12 + place] = 1
    return [jnp.asarray(t, BF16) for t in (np.stack(picks), order, pack)]


def arrange_table():
    table = np.zeros((384, 432), np.float32)
    for lev in range(LEV):
        for lanes in range(4):
            for col in range(48):
                device, place = divmod(col, 6)
                source, patch = (device, 3 + place) if place < 3 else (device + 1, place - 3)
                piece = source * 48 + lanes * 12 + lev * 6 + patch
                table[(lev * 4 + lanes) * 48 + col, piece] = 1
    return jnp.asarray(table, BF16)


def dot(a, b):
    return jnp.dot(a, b, preferred_element_type=F32)


def dot_nt(a, b):
    return lax.dot_general(a, b, (((1,), (1,)), ((), ())), preferred_element_type=F32)


def normalize(values):
    center = values - jnp.mean(values, -1, keepdims=True)
    spread = jnp.mean(center * center, -1, keepdims=True)
    return center * lax.rsqrt(spread + 1e-05)


def fused(
    n_lat,
    n_lon,
    tokens,
    region,
    pick,
    order,
    pack,
    w_qkv_hbm,
    w_out_hbm,
    w_merge_hbm,
    recv,
    own,
    east,
    own_region,
    east_region,
    own_next,
    east_next,
    own_marks,
    east_marks,
    stage,
    w_qk,
    w_v,
    w_vt,
    w_out,
    w_merge,
    xs,
    ns,
    ms,
    qs,
    ks,
    wos,
    carry,
    odd_save,
    carry_send,
    carry_recv,
    load_sems,
    row_send,
    row_recv,
    halo_send,
    halo_recv,
    carry_sems,
    out_send,
    out_recv,
):
    lat = lax.axis_index("lat")
    lon = lax.axis_index("lon")
    next_lat = lax.rem(lat + 1, n_lat)
    prev_lat = lax.rem(lat + n_lat - 1, n_lat)
    west_lon = lax.rem(lon + n_lon - 1, n_lon)
    east_lon = lax.rem(lon + 1, n_lon)
    rows = tokens.shape[2] * 8
    channels = tokens.shape[4]
    windows = rows // WIN_LAT
    chunks = windows // GROUP
    pairs = chunks // 2
    blocks16 = rows // 16
    first_pair = lax.rem((lon * pairs) // n_lon, pairs)
    first = 2 * first_pair
    first_west = lax.rem((west_lon * pairs) // n_lon, pairs)

    loads = [
        pltpu.make_async_copy(tokens.at[:, 6:12], own.at[:, :, : rows // 8], load_sems.at[0]),
        pltpu.make_async_copy(region.at[6:12], own_region, load_sems.at[1]),
        pltpu.make_async_copy(w_qkv_hbm.at[:, : 2 * channels], w_qk, load_sems.at[2]),
        pltpu.make_async_copy(w_qkv_hbm.at[:, 2 * channels :], w_v, load_sems.at[3]),
        pltpu.make_async_copy(w_out_hbm, w_out, load_sems.at[4]),
        pltpu.make_async_copy(w_merge_hbm, w_merge, load_sems.at[5]),
    ]
    for load in loads:
        load.start()

    barrier = pltpu.get_barrier_semaphore()

    def greet(step, _):
        other = lax.rem(lon + step, n_lon)
        pl.semaphore_signal(barrier, inc=1, device_id=(lat, other), device_id_type=MESH)
        return 0

    lax.fori_loop(1, n_lon, greet, 0)
    pl.semaphore_signal(barrier, inc=1, device_id=(prev_lat, lon), device_id_type=MESH)
    pl.semaphore_signal(barrier, inc=1, device_id=(next_lat, lon), device_id_type=MESH)
    pl.semaphore_signal(barrier, inc=1, device_id=(next_lat, east_lon), device_id_type=MESH)

    @pl.when(lon == 0)
    def _():
        def greet_before(other, _):
            pl.semaphore_signal(barrier, inc=1, device_id=(prev_lat, other), device_id_type=MESH)
            return 0

        lax.fori_loop(0, n_lon, greet_before, 0)

    pl.semaphore_wait(barrier, n_lon + 3)

    def remote(source, target, send_sem, recv_sem, device):
        return pltpu.make_async_remote_copy(
            src_ref=source,
            dst_ref=target,
            send_sem=send_sem,
            recv_sem=recv_sem,
            device_id=device,
            device_id_type=MESH,
        )

    def halo_copy(block):
        part = pl.ds(block * 2, 2)
        return remote(
            tokens.at[:, 0:6, part],
            east.at[:, :, part],
            halo_send.at[block],
            halo_recv.at[block],
            (lat, west_lon),
        )

    def send_west(step, _):
        halo_copy(lax.rem(3 * first_west + step, blocks16)).start()
        return 0

    next_rows = pl.ds(rows // 8, 1)
    ahead = [
        remote(region.at[0:6], east_region, row_send.at[0], row_recv.at[0], (lat, west_lon)),
        remote(
            region.at[6:12, :, :128], own_next, row_send.at[1], row_recv.at[1], (prev_lat, lon)
        ),
        remote(
            region.at[0:6, :, :128],
            east_next,
            row_send.at[2],
            row_recv.at[2],
            (prev_lat, west_lon),
        ),
        remote(
            tokens.at[:, 6:12, 0:1],
            own.at[:, :, next_rows],
            row_send.at[3],
            row_recv.at[3],
            (prev_lat, lon),
        ),
        remote(
            tokens.at[:, 0:6, 0:1],
            east.at[:, :, next_rows],
            row_send.at[4],
            row_recv.at[4],
            (prev_lat, west_lon),
        ),
    ]
    for copy in ahead[:3]:
        copy.start()
    lax.fori_loop(0, 4, send_west, 0)
    for copy in ahead[3:]:
        copy.start()
    lax.fori_loop(4, blocks16, send_west, 0)

    def eye(size):
        row = lax.broadcasted_iota(jnp.int32, (size, size), 0)
        return (row == lax.broadcasted_iota(jnp.int32, (size, size), 1)).astype(F32).astype(BF16)

    def one_hot(lane_labels):
        label = lax.broadcasted_iota(jnp.int32, (128, lane_labels.shape[1]), 0)
        return (label == lane_labels).astype(F32).astype(BF16)

    pole = (lat == n_lat - 1).astype(jnp.int32)
    row_eye = eye(rows)
    next_eye = eye(128)[:8]

    def mark_half(here, after, marks):
        def mark_column(col, _):
            for lev in range(LEV):
                labels = here[col, lev : lev + 1] * 2
                marks[lev, col, pl.ds(0, rows // 8)] = (
                    dot_nt(row_eye, one_hot(labels)).astype(BF16).reshape(rows // 8, 8, 128)
                )
                labels = after[col, lev : lev + 1] * 2 + pole
                marks[lev, col, rows // 8] = dot_nt(next_eye, one_hot(labels)).astype(BF16)
            return 0

        lax.fori_loop(0, 6, mark_column, 0)

    loads[1].wait()
    ahead[1].wait_recv()
    mark_half(own_region, own_next, own_marks)
    loads[3].wait()
    w_vt[...] = dot_nt(eye(channels), w_v[...]).astype(BF16)
    ahead[0].wait_recv()
    ahead[2].wait_recv()
    mark_half(east_region, east_next, east_marks)
    for load in (loads[0], loads[2], loads[4], loads[5]):
        load.wait()

    score_scale = 32 ** (-0.5) * 1.4426950408889634
    head_of_lane = lax.broadcasted_iota(jnp.int32, (SPAN, 128), 1) // 32
    head_of_row = lax.broadcasted_iota(jnp.int32, (128, 128), 0) // 32
    tail_head = lax.broadcasted_iota(jnp.int32, (128, 64), 1) // 16
    tail_row = lax.broadcasted_iota(jnp.int32, (128, 64), 0) // 32
    sum_row = lax.broadcasted_iota(jnp.int32, (16, 512), 0)
    sum_lane = lax.broadcasted_iota(jnp.int32, (16, 512), 1) // 128
    tail_sum_row = lax.broadcasted_iota(jnp.int32, (16, 64), 0)
    tail_sum_lane = lax.broadcasted_iota(jnp.int32, (16, 64), 1) // 16
    sum_rows = jnp.concatenate(
        [(sum_row == sum_lane).astype(F32), (tail_sum_row == tail_sum_lane).astype(F32)], 1
    ).astype(BF16)
    def stacked(value):
        return jnp.concatenate([value[:128]] * 4 + [value[128:]] * 4, 0)

    def window_parts(i):
        normed = ns[pl.ds(i * SPAN, SPAN)]
        value_t = dot_nt(
            w_vt[...], jnp.concatenate([normed[:128]] + [normed[128:]] * 4, 0)
        ).astype(BF16)
        marks = ms[pl.ds(i * SPAN, SPAN)]
        key_marks = stacked(((marks.astype(F32) - 1.0) * 1e30).astype(BF16))
        return value_t, marks, key_marks

    def scores_of(i, g, parts):
        base = i * SPAN
        lanes = pl.ds(g * 128, 128)
        query = jnp.concatenate([qs[pl.ds(base, SPAN), lanes], parts[1]], 1)
        key = ks[pl.ds(base, SPAN), lanes]
        heads = [jnp.where(head_of_lane == h, key, jnp.zeros_like(key)) for h in range(4)]
        keys = jnp.concatenate([k[:128] for k in heads] + [k[128:] for k in heads], 0)
        return dot_nt(jnp.concatenate([keys, parts[2]], 1), query)

    def weights_of(scores):
        mains, tails = [], []
        for h in range(4):
            main = scores[128 * h : 128 * h + 128]
            tail = scores[512 + 16 * h : 528 + 16 * h]
            peak = jnp.maximum(jnp.max(main, 0, keepdims=True), jnp.max(tail, 0, keepdims=True))
            mains.append(jnp.exp2((main - peak).astype(BF16)))
            tails.append(jnp.exp2((tail - peak).astype(BF16)))
        return jnp.concatenate(mains + tails, 0)

    def outs_of(g, parts, weights):
        group_values = parts[0][g * 128 : g * 128 + 128]
        main_values = group_values[:, :128]
        tail_values = group_values[:, 128:192]
        blocks = [
            jnp.where(head_of_row == h, main_values, jnp.zeros_like(main_values)) for h in range(4)
        ]
        blocks.append(jnp.where(tail_head == tail_row, tail_values, jnp.zeros_like(tail_values)))
        values = jnp.concatenate([jnp.concatenate(blocks, 1), sum_rows], 0)
        result = dot(values, weights)
        scale = 1.0 / result[128:136]
        return [result[32 * h : 32 * h + 32] * scale[h : h + 1] for h in range(4)]

    def attend_chunk():
        groups = HEADS // 4
        count = GROUP * groups
        parts, scores, weights, outs = {}, {}, {}, {i: [] for i in range(GROUP)}
        for t in range(count + 2):
            if t < count:
                i, g = divmod(t, groups)
                if g == 0:
                    parts[i] = window_parts(i)
                scores[t] = scores_of(i, g, parts[i])
            if 0 <= t - 2 < count:
                i, g = divmod(t - 2, groups)
                outs[i] += outs_of(g, parts[i], weights.pop(t - 2))
                if g == groups - 1:
                    out_t = jnp.concatenate(outs.pop(i), 0).astype(BF16)
                    wos[pl.ds(i * PADDED, PADDED)] = dot_nt(order[...], out_t).astype(BF16)
            if 0 <= t - 1 < count:
                weights[t - 1] = weights_of(scores.pop(t - 1))

    def merge(blocks):
        total = sum(jnp.sum(b, -1, keepdims=True) for b in blocks)
        mean = total * (1.0 / 2048)
        blocks = [b - mean for b in blocks]
        spread = sum(jnp.sum(b * b, -1, keepdims=True) for b in blocks) * (1.0 / 2048)
        factor = lax.rsqrt(spread + 1e-05)
        merge_in = jnp.concatenate([(b * factor).astype(BF16) for b in blocks], 1)
        return dot(merge_in, w_merge[...])

    def packed(rows40):
        stacked_lanes = jnp.concatenate([rows40[:, 256 * j : 256 * j + 256] for j in range(4)], 0)
        return dot(pack[...], stacked_lanes.astype(BF16)).astype(BF16)

    def own_copy():
        return pltpu.make_async_copy(
            stage.at[pl.ds(3 * lon, 3)], recv.at[lon], out_recv
        )

    def send_copy(owner):
        return pltpu.make_async_remote_copy(
            src_ref=stage.at[pl.ds(3 * owner, 3)],
            dst_ref=recv.at[lon],
            send_sem=out_send.at[owner],
            recv_sem=out_recv,
            device_id=(lat, owner),
            device_id_type=MESH,
        )

    def own_zero_copy():
        return pltpu.make_async_copy(
            stage.at[pl.ds(1, 2)], recv.at[lon, pl.ds(1, 2)], out_recv
        )

    def send_zero_copy():
        return pltpu.make_async_remote_copy(
            src_ref=stage.at[pl.ds(1, 2)],
            dst_ref=recv.at[lon, pl.ds(1, 2)],
            send_sem=out_send.at[0],
            recv_sem=out_recv,
            device_id=(lat, 0),
            device_id_type=MESH,
        )

    def last_copy():
        return pltpu.make_async_remote_copy(
            src_ref=stage.at[pl.ds(3 * windows, 1)],
            dst_ref=recv.at[lon, pl.ds(0, 1)],
            send_sem=out_send.at[windows],
            recv_sem=out_recv,
            device_id=(next_lat, 0),
            device_id_type=MESH,
        )

    def send(owner):
        @pl.when(owner == lon)
        def _():
            own_copy().start()

        @pl.when(owner != lon)
        def _():
            send_copy(owner).start()

    carry_copy = pltpu.make_async_remote_copy(
        src_ref=carry_send,
        dst_ref=carry_recv,
        send_sem=carry_sems.at[0],
        recv_sem=carry_sems.at[1],
        device_id=(next_lat, lon),
        device_id_type=MESH,
    )

    carry[...] = jnp.zeros_like(carry)
    slot_row = lax.broadcasted_iota(jnp.int32, (GROUP * 40, 512), 0) % 40 < 12

    def chunk_step(step, _):
        chunk = lax.rem(first + step, chunks)
        start = chunk * GROUP

        pair = chunk // 2
        even = chunk == 2 * pair

        @pl.when(jnp.logical_and(even, jnp.logical_or(step == 0, pair == 0)))
        def _():
            halo_copy(3 * pair).wait_recv()

        @pl.when(even)
        def _():
            halo_copy(3 * pair + 1).wait_recv()

        @pl.when(jnp.logical_not(even))
        def _():
            halo_copy(3 * pair + 2).wait_recv()

            @pl.when(jnp.logical_and(pair != pairs - 1, pair + 1 != first_pair))
            def _():
                halo_copy(3 * pair + 3).wait_recv()

            @pl.when(pair == pairs - 1)
            def _():
                ahead[3].wait_recv()
                ahead[4].wait_recv()

        for i in range(GROUP):
            part = pl.ds(3 * chunk + PICK_STARTS[i], 2)
            raw = [
                jnp.concatenate(
                    [value[:, :, part].reshape(BLOCK, channels), marks[:, :, part].reshape(BLOCK, 128)],
                    1,
                )
                for value, marks in ((own, own_marks), (east, east_marks))
            ]
            value = dot(pick[i], jnp.concatenate(raw, 0))
            ms[pl.ds(i * SPAN, SPAN)] = value[:, channels:].astype(BF16)
            value = value[:, :channels]
            xs[pl.ds(i * SPAN, SPAN)] = value.astype(BF16)
            ns[pl.ds(i * SPAN, SPAN)] = normalize(value).astype(BF16)
        qs[...] = (dot(ns[...], w_qk[:, :512]) * score_scale).astype(BF16)
        ks[...] = dot(ns[...], w_qk[:, 512:]).astype(BF16)
        attend_chunk()
        residual = jnp.concatenate(
            [dot(order[...], xs[pl.ds(i * SPAN, SPAN)]) for i in range(GROUP)], 0
        )
        updated = (residual + dot(wos[...], w_out[...])).astype(BF16).astype(F32)
        blocks = []
        for p in range(4):
            pieces = [
                updated[PADDED * i + 40 * p : PADDED * i + 40 * p + 40] for i in range(GROUP)
            ]
            block = jnp.concatenate(pieces, 0)
            if p < 2:
                before = jnp.concatenate([carry[pl.ds(40 * p, 40)]] + pieces[:-1], 0)
                carry[pl.ds(40 * p, 40)] = pieces[-1]
                block = jnp.where(slot_row, before, block)
            blocks.append(block)

        @pl.when(step == 0)
        def _():
            for p in range(2):
                odd_save[1, pl.ds(16 * p, 16)] = blocks[2 + p][:16]

        @pl.when(chunk == 0)
        def _():
            for p in range(2):
                odd_save[0, pl.ds(16 * p, 16)] = blocks[2 + p][:16]

        @pl.when(chunk == chunks - 1)
        def _():
            for p in range(2):
                carry_send[pl.ds(16 * p, 16)] = carry[pl.ds(40 * p, 16)].astype(BF16)
            carry_copy.start()

        merged = merge(blocks)
        for i in range(GROUP):
            pieces = packed(merged[40 * i : 40 * i + 40])
            for slot in range(3):
                stage[3 * (start + i) + 1 + slot] = pieces[48 * slot : 48 * slot + 48]
            owner = start + i
            if i == 0:

                @pl.when(jnp.logical_and(step > 0, chunk > 0))
                def _():
                    send(owner)
            else:
                send(owner)

        @pl.when(chunk == chunks - 1)
        def _():
            last_copy().start()

        return 0

    lax.fori_loop(0, chunks, chunk_step, 0)

    carry_copy.wait_recv()
    lat_carry = carry_recv[...].astype(F32)
    blocks = []
    for p in range(2):
        blocks.append(
            jnp.concatenate([lat_carry[16 * p : 16 * p + 16], carry[pl.ds(40 * p, 16)]], 0)
        )
    for p in range(2):
        blocks.append(
            jnp.concatenate([odd_save[0, pl.ds(16 * p, 16)], odd_save[1, pl.ds(16 * p, 16)]], 0)
        )
    merged = merge(blocks)
    zero_rows = jnp.zeros((24, merged.shape[1]), F32)
    stage[1] = packed(jnp.concatenate([merged[:16], zero_rows], 0))[:48]

    @pl.when(lon == 0)
    def _():
        own_zero_copy().start()

    @pl.when(lon != 0)
    def _():
        send_zero_copy().start()

    @pl.when(first != 0)
    def _():
        stage[3 * GROUP * first + 1] = packed(jnp.concatenate([merged[16:], zero_rows], 0))[:48]
        send(GROUP * first)

    def wait_halo(block, _):
        halo_copy(block).wait_send()
        return 0

    lax.fori_loop(0, blocks16, wait_halo, 0)
    for copy in ahead:
        copy.wait_send()
    carry_copy.wait_send()
    last_copy().wait_send()

    @pl.when(lon != 0)
    def _():
        send_zero_copy().wait_send()

    def wait_send(owner, _):
        @pl.when(owner != lon)
        def _():
            send_copy(owner).wait_send()

        return 0

    lax.fori_loop(1, windows, wait_send, 0)
    pltpu.make_async_copy(recv, recv, out_recv).wait()


def exchange(tokens, region, w_qkv, w_out, w_merge, n_lat, n_lon):
    levels, cols, tiles, _, channels = tokens.shape
    rows = tiles * 8
    windows = rows // WIN_LAT
    vmem = pl.BlockSpec(memory_space=pltpu.VMEM)
    hbm = pl.BlockSpec(memory_space=pl.ANY)
    span = GROUP * SPAN
    half = cols // 2
    return pl.pallas_call(
        functools.partial(fused, n_lat, n_lon),
        out_shape=jax.ShapeDtypeStruct((n_lon, 3, 48, 256), BF16),
        in_specs=[hbm] * 2 + [vmem] * 3 + [hbm] * 3,
        out_specs=hbm,
        scratch_shapes=[
            pltpu.VMEM((levels, half, tiles + 1, 8, channels), BF16),
            pltpu.VMEM((levels, half, tiles + 1, 8, channels), BF16),
            pltpu.VMEM((half, levels, rows), jnp.int32),
            pltpu.VMEM((half, levels, rows), jnp.int32),
            pltpu.VMEM((half, levels, 128), jnp.int32),
            pltpu.VMEM((half, levels, 128), jnp.int32),
            pltpu.VMEM((levels, half, tiles + 1, 8, 128), BF16),
            pltpu.VMEM((levels, half, tiles + 1, 8, 128), BF16),
            pltpu.VMEM((3 * windows + 1, 48, 256), BF16),
            pltpu.VMEM((channels, 2 * channels), BF16),
            pltpu.VMEM((channels, channels), BF16),
            pltpu.VMEM((channels, channels), BF16),
            pltpu.VMEM((channels, channels), BF16),
            pltpu.VMEM((4 * channels, 2 * channels), BF16),
            pltpu.VMEM((span, channels), BF16),
            pltpu.VMEM((span, channels), BF16),
            pltpu.VMEM((span, 128), BF16),
            pltpu.VMEM((span, channels), BF16),
            pltpu.VMEM((span, channels), BF16),
            pltpu.VMEM((GROUP * PADDED, channels), BF16),
            pltpu.VMEM((80, channels), F32),
            pltpu.VMEM((2, 32, channels), F32),
            pltpu.VMEM((32, channels), BF16),
            pltpu.VMEM((32, channels), BF16),
            pltpu.SemaphoreType.DMA((6,)),
            pltpu.SemaphoreType.DMA((5,)),
            pltpu.SemaphoreType.DMA((5,)),
            pltpu.SemaphoreType.DMA((rows // 16,)),
            pltpu.SemaphoreType.DMA((rows // 16,)),
            pltpu.SemaphoreType.DMA((2,)),
            pltpu.SemaphoreType.DMA((windows + 1,)),
            pltpu.SemaphoreType.DMA,
        ],
        compiler_params=pltpu.CompilerParams(
            collective_id=0, has_side_effects=True, vmem_limit_bytes=56 * 1024 * 1024
        ),
        name="attend_merge_send",
    )(tokens, region, *tables(), w_qkv, w_out, w_merge)


def place(table, pieces, out):
    sources = pieces.shape[0]
    for group in range(sources // 8):
        before = pieces[(8 * group + sources - 1) % sources, 0]
        here = pieces[8 * group : 8 * group + 8, 0].reshape(384, 256)
        columns = dot(table[...], jnp.concatenate([before, here], 0)).astype(BF16)
        for lev in range(LEV):
            for lanes in range(4):
                at = (lev * 4 + lanes) * 48
                out[lev, 0, 48 * group : 48 * group + 48, 256 * lanes : 256 * lanes + 256] = (
                    columns[at : at + 48]
                )


def arrange(recv):
    n_lon = recv.shape[0]
    return pl.pallas_call(
        place,
        grid=(3,),
        out_shape=jax.ShapeDtypeStruct((LEV, 3, n_lon * 6, 1024), BF16),
        in_specs=[
            pl.BlockSpec((384, 432), lambda row: (0, 0)),
            pl.BlockSpec((n_lon, 1, 48, 256), lambda row: (0, row, 0, 0)),
        ],
        out_specs=pl.BlockSpec((LEV, 1, n_lon * 6, 1024), lambda row: (0, row, 0, 0)),
        name="place_columns",
    )(arrange_table(), recv)


def solution(mesh):
    n_lat, n_lon = mesh.shape["lat"], mesh.shape["lon"]

    def body(tokens, region, w_qkv, w_out, w_merge):
        levels, rows, cols, channels = tokens.shape
        by_column = tokens.transpose(0, 2, 1, 3).reshape(levels, cols, rows // 8, 8, channels)
        recv = exchange(
            by_column, region.transpose(2, 0, 1), w_qkv, w_out, w_merge, n_lat, n_lon
        )
        return arrange(recv)

    in_specs = (P(None, "lat", "lon", None), P(None, "lat", "lon"), P(), P(), P())
    out_specs = P(None, ("lat", "lon"), None, None)
    return jax.shard_map(body, mesh=mesh, in_specs=in_specs, out_specs=out_specs, check_vma=False)
```

time: 157 us -> 110 us (0.70)
  local copies, waits for them, and re-layouts: 18.7 us -> 0 us
  Pallas kernels: 124 us -> 109 us
  starting transfers between devices: 9.15 us -> 0 us
  other arithmetic: 2.53 us -> 0 us
    pallas_call x1, Pallas kernels: 124 us -> 104 us  [exchange(): pl.pallas_call(functools.partial(fused, n_lat, n_lon), out_shape=jax.Shap...]
    ppermute x2 -> x0, starting transfers between devices: 9.15 us -> none  [shifted(): return lax.ppermute(value, axis, pairs)]
    unnamed x4 -> x0, local copies, waits for them, and re-layouts: 8.93 us -> none
    pallas_call x0 -> x1, Pallas kernels: none -> 4.72 us  [arrange(): pl.pallas_call(place, grid=(3,), out_shape=jax.ShapeDtypeStruct((LEV, 3,...]
    reshape x2 -> x0, local copies, waits for them, and re-layouts: 3.27 us -> none  [the longest x1 2.89 us: arrange(): return parts.reshape(LEV, 3, n_lon * 6, 1024)]
    pallas_call x1 -> x0, local copies, waits for them, and re-layouts: 2.52 us -> none  [exchange(): pl.pallas_call(functools.partial(fused, n_lat, n_lon), out_shape=jax.Shap...]
    slice x13 -> x0, local copies, waits for them, and re-layouts: 1.95 us -> none  [the longest x1 1.12 us: exchange(): w_qk = w_qkv[:, :2 * channels]]
    transpose x1 -> x0, local copies, waits for them, and re-layouts: 1.83 us -> none  [arrange(): parts = parts.transpose(3, 1, 0, 4, 5, 2, 6)]
  transfers between devices with their start and end apart: 2 -> 0, of which waited for: 1 -> 0; matrix products, arithmetic and copies ran while one was open for 7% -> 0% of each run, Pallas kernels for 0% -> 0%
where the time goes in v2:
time: 110 us; the launch traced here: 109 us
  Pallas kernels  109 us (99%)
    pallas_call x1, Pallas kernels, exchange(): pl.pallas_call(functools.partial(fused, n_lat, n_lon), out_shape=jax.Shap...  104 us
    pallas_call x1, Pallas kernels, arrange(): pl.pallas_call(place, grid=(3,), out_shape=jax.ShapeDtypeStruct((LEV, 3,...  4.72 us

profile of v2, /device:TPU:0, one launch (start us, length us, event | category | flops | bytes accessed | tf_op | source)
XLA Modules:
  0.0 109.1 jit_solution(17488614543525528934)
XLA Ops:
  0.0 104.4 %attend_merge_send.1.pieces = bf16[32,3,48,256]{3,2,1,0:T(8,128)(2,1)} custom-call(bf16[2,12,24,8,512]{4,3,2,1,0:T(8,128)(2,1)} %bitcast.4, s32[12,2,192]{2,1,0:T(2,128)} %bitcast.5, bf16[4,144,384]{2,1,0:T(8,128)(2,1)} %constant.8.clone.pick, bf16[160,144]{1,0:T(8,128)(2,1)} %constant.9.clone.order, bf16[144,160]{1,0:T(8,128)(2,1)} %constant.10.clone.pack, ...), custom_call_target="tpu_custom_call" | custom-call | tf_op jit(solution)/shard_map/attend_merge_send/pallas_call | solution.py:579
  104.4 4.7 %place_columns.1 = bf16[2,3,192,1024]{3,2,1,0:T(8,128)(2,1)} custom-call(bf16[384,432]{1,0:T(8,128)(2,1)} %constant.11.clone.table, bf16[32,3,48,256]{3,2,1,0:T(8,128)(2,1)} %attend_merge_send.1.pieces), custom_call_target="tpu_custom_call" | custom-call | tf_op jit(solution)/shard_map/place_columns/pallas_call | solution.py:641

commit v3 on v2

--- a/solution.py
+++ b/solution.py
@@ -26,7 +26,7 @@
 def tables():
     pick = np.zeros((SPAN, 2 * BLOCK), np.float32)
     order = np.zeros((PADDED, SPAN), np.float32)
-    pack = np.zeros((SPAN, PADDED), np.float32)
+    pack = np.zeros((SPAN // 2, PADDED // 2), np.float32)
     picks = []
     for offset in PICK_ROWS:
         pick = np.zeros((SPAN, 2 * BLOCK), np.float32)
@@ -46,21 +46,21 @@
                         token = line * 6 + window_rows[odd][slot]
                         order[block * 40 + slot * 12 + lev * 6 + patch, token] = 1
     for slot in range(3):
-        for lanes in range(4):
+        for lanes in range(2):
             for place in range(12):
-                pack[slot * 48 + lanes * 12 + place, lanes * 40 + slot * 12 + place] = 1
+                pack[slot * 24 + lanes * 12 + place, lanes * 40 + slot * 12 + place] = 1
     return [jnp.asarray(t, BF16) for t in (np.stack(picks), order, pack)]
 
 
 def arrange_table():
-    table = np.zeros((384, 432), np.float32)
+    table = np.zeros((192, 216), np.float32)
     for lev in range(LEV):
-        for lanes in range(4):
+        for lanes in range(2):
             for col in range(48):
                 device, place = divmod(col, 6)
                 source, patch = (device, 3 + place) if place < 3 else (device + 1, place - 3)
-                piece = source * 48 + lanes * 12 + lev * 6 + patch
-                table[(lev * 4 + lanes) * 48 + col, piece] = 1
+                piece = source * 24 + lanes * 12 + lev * 6 + patch
+                table[(lev * 2 + lanes) * 48 + col, piece] = 1
     return jnp.asarray(table, BF16)
 
 
@@ -133,11 +133,12 @@
     channels = tokens.shape[4]
     windows = rows // WIN_LAT
     chunks = windows // GROUP
-    pairs = chunks // 2
-    blocks16 = rows // 16
-    first_pair = lax.rem((lon * pairs) // n_lon, pairs)
-    first = 2 * first_pair
-    first_west = lax.rem((west_lon * pairs) // n_lon, pairs)
+
+    def first_chunk(place):
+        return (place // 8) * (chunks // 4)
+
+    first = first_chunk(lon)
+    first_west = first_chunk(west_lon)
 
     loads = [
         pltpu.make_async_copy(tokens.at[:, 6:12], own.at[:, :, : rows // 8], load_sems.at[0]),
@@ -182,18 +183,29 @@
             device_id_type=MESH,
         )
 
-    def halo_copy(block):
-        part = pl.ds(block * 2, 2)
+    def halo_copy(chunk, start, count):
+        part = pl.ds(start, count)
         return remote(
             tokens.at[:, 0:6, part],
             east.at[:, :, part],
-            halo_send.at[block],
-            halo_recv.at[block],
+            halo_send.at[chunk],
+            halo_recv.at[chunk],
             (lat, west_lon),
         )
 
+    def halo_case(chunk, start_chunk, act):
+        head = jnp.logical_or(chunk == start_chunk, chunk == 0)
+        short = jnp.logical_or(chunk == chunks - 1, chunk + 1 == start_chunk)
+        for is_head in (False, True):
+            for is_short in (False, True):
+
+                @pl.when(jnp.logical_and(head == is_head, short == is_short))
+                def _():
+                    count = 3 + int(is_head) - int(is_short)
+                    act(halo_copy(chunk, 3 * chunk + 1 - int(is_head), count))
+
     def send_west(step, _):
-        halo_copy(lax.rem(3 * first_west + step, blocks16)).start()
+        halo_case(lax.rem(first_west + step, chunks), first_west, lambda copy: copy.start())
         return 0
 
     next_rows = pl.ds(rows // 8, 1)
@@ -226,10 +238,10 @@
     ]
     for copy in ahead[:3]:
         copy.start()
-    lax.fori_loop(0, 4, send_west, 0)
+    lax.fori_loop(0, 2, send_west, 0)
     for copy in ahead[3:]:
         copy.start()
-    lax.fori_loop(4, blocks16, send_west, 0)
+    lax.fori_loop(2, chunks, send_west, 0)
 
     def eye(size):
         row = lax.broadcasted_iota(jnp.int32, (size, size), 0)
@@ -352,7 +364,7 @@
         return dot(merge_in, w_merge[...])
 
     def packed(rows40):
-        stacked_lanes = jnp.concatenate([rows40[:, 256 * j : 256 * j + 256] for j in range(4)], 0)
+        stacked_lanes = jnp.concatenate([rows40[:, 512 * j : 512 * j + 512] for j in range(2)], 0)
         return dot(pack[...], stacked_lanes.astype(BF16)).astype(BF16)
 
     def own_copy():
@@ -370,20 +382,28 @@
             device_id_type=MESH,
         )
 
-    def own_zero_copy():
+    def own_part(place, target, count):
         return pltpu.make_async_copy(
-            stage.at[pl.ds(1, 2)], recv.at[lon, pl.ds(1, 2)], out_recv
-        )
-
-    def send_zero_copy():
-        return pltpu.make_async_remote_copy(
-            src_ref=stage.at[pl.ds(1, 2)],
-            dst_ref=recv.at[lon, pl.ds(1, 2)],
-            send_sem=out_send.at[0],
-            recv_sem=out_recv,
-            device_id=(lat, 0),
-            device_id_type=MESH,
-        )
+            stage.at[pl.ds(place, count)], recv.at[lon, pl.ds(target, count)], out_recv
+        )
+
+    def send_part(owner, place, target, count, sem):
+        return remote(
+            stage.at[pl.ds(place, count)],
+            recv.at[lon, pl.ds(target, count)],
+            out_send.at[sem],
+            out_recv,
+            (lat, owner),
+        )
+
+    def part_of(owner, place, target, count, sem):
+        @pl.when(owner == lon)
+        def _():
+            own_part(place, target, count).start()
+
+        @pl.when(owner != lon)
+        def _():
+            send_part(owner, place, target, count, sem).start()
 
     def last_copy():
         return pltpu.make_async_remote_copy(
@@ -420,29 +440,12 @@
         chunk = lax.rem(first + step, chunks)
         start = chunk * GROUP
 
-        pair = chunk // 2
-        even = chunk == 2 * pair
-
-        @pl.when(jnp.logical_and(even, jnp.logical_or(step == 0, pair == 0)))
-        def _():
-            halo_copy(3 * pair).wait_recv()
-
-        @pl.when(even)
-        def _():
-            halo_copy(3 * pair + 1).wait_recv()
-
-        @pl.when(jnp.logical_not(even))
-        def _():
-            halo_copy(3 * pair + 2).wait_recv()
-
-            @pl.when(jnp.logical_and(pair != pairs - 1, pair + 1 != first_pair))
-            def _():
-                halo_copy(3 * pair + 3).wait_recv()
-
-            @pl.when(pair == pairs - 1)
-            def _():
-                ahead[3].wait_recv()
-                ahead[4].wait_recv()
+        halo_case(chunk, first, lambda copy: copy.wait_recv())
+
+        @pl.when(chunk == chunks - 1)
+        def _():
+            ahead[3].wait_recv()
+            ahead[4].wait_recv()
 
         for i in range(GROUP):
             part = pl.ds(3 * chunk + PICK_STARTS[i], 2)
@@ -497,13 +500,21 @@
         for i in range(GROUP):
             pieces = packed(merged[40 * i : 40 * i + 40])
             for slot in range(3):
-                stage[3 * (start + i) + 1 + slot] = pieces[48 * slot : 48 * slot + 48]
+                stage[3 * (start + i) + 1 + slot] = pieces[24 * slot : 24 * slot + 24].reshape(3, 8, 512)
             owner = start + i
             if i == 0:
 
                 @pl.when(jnp.logical_and(step > 0, chunk > 0))
                 def _():
                     send(owner)
+
+                @pl.when(chunk == 0)
+                def _():
+                    part_of(0, 2, 2, 1, 0)
+
+                @pl.when(jnp.logical_and(step == 0, chunk > 0))
+                def _():
+                    part_of(owner, 3 * owner + 2, 2, 1, owner)
             else:
                 send(owner)
 
@@ -517,37 +528,28 @@
 
     carry_copy.wait_recv()
     lat_carry = carry_recv[...].astype(F32)
-    blocks = []
-    for p in range(2):
-        blocks.append(
-            jnp.concatenate([lat_carry[16 * p : 16 * p + 16], carry[pl.ds(40 * p, 16)]], 0)
-        )
-    for p in range(2):
-        blocks.append(
-            jnp.concatenate([odd_save[0, pl.ds(16 * p, 16)], odd_save[1, pl.ds(16 * p, 16)]], 0)
-        )
-    merged = merge(blocks)
-    zero_rows = jnp.zeros((24, merged.shape[1]), F32)
-    stage[1] = packed(jnp.concatenate([merged[:16], zero_rows], 0))[:48]
-
-    @pl.when(lon == 0)
-    def _():
-        own_zero_copy().start()
-
-    @pl.when(lon != 0)
-    def _():
-        send_zero_copy().start()
+    rows_of = lambda p: pl.ds(16 * p, 16)
+    pieces = [
+        jnp.concatenate([lat_carry[16 * p : 16 * p + 16], carry[pl.ds(40 * p, 16)]], 0)
+        for p in range(2)
+    ]
+    pieces += [jnp.concatenate([odd_save[0, rows_of(p)], odd_save[1, rows_of(p)]], 0) for p in range(2)]
+    merged = merge(pieces)
+    zero_rows = jnp.zeros((24, 2 * channels), F32)
+    stage[1] = packed(jnp.concatenate([merged[:16], zero_rows], 0))[:24].reshape(3, 8, 512)
+    part_of(0, 1, 1, 1, windows + 1)
+    split = GROUP * first
 
     @pl.when(first != 0)
     def _():
-        stage[3 * GROUP * first + 1] = packed(jnp.concatenate([merged[16:], zero_rows], 0))[:48]
-        send(GROUP * first)
-
-    def wait_halo(block, _):
-        halo_copy(block).wait_send()
+        stage[3 * split + 1] = packed(jnp.concatenate([merged[16:], zero_rows], 0))[:24].reshape(3, 8, 512)
+        part_of(split, 3 * split, 0, 2, windows + 2)
+
+    def wait_halo(chunk, _):
+        halo_case(chunk, first_west, lambda copy: copy.wait_send())
         return 0
 
-    lax.fori_loop(0, blocks16, wait_halo, 0)
+    lax.fori_loop(0, chunks, wait_halo, 0)
     for copy in ahead:
         copy.wait_send()
     carry_copy.wait_send()
@@ -555,10 +557,16 @@
 
     @pl.when(lon != 0)
     def _():
-        send_zero_copy().wait_send()
+        send_part(0, 2, 2, 1, 0).wait_send()
+        send_part(0, 1, 1, 1, windows + 1).wait_send()
+
+    @pl.when(jnp.logical_and(first != 0, split != lon))
+    def _():
+        send_part(split, 3 * split + 2, 2, 1, split).wait_send()
+        send_part(split, 3 * split, 0, 2, windows + 2).wait_send()
 
     def wait_send(owner, _):
-        @pl.when(owner != lon)
+        @pl.when(jnp.logical_and(owner != lon, owner != split))
         def _():
             send_copy(owner).wait_send()
 
@@ -578,7 +586,7 @@
     half = cols // 2
     return pl.pallas_call(
         functools.partial(fused, n_lat, n_lon),
-        out_shape=jax.ShapeDtypeStruct((n_lon, 3, 48, 256), BF16),
+        out_shape=jax.ShapeDtypeStruct((n_lon, 3, 3, 8, 512), BF16),
         in_specs=[hbm] * 2 + [vmem] * 3 + [hbm] * 3,
         out_specs=hbm,
         scratch_shapes=[
@@ -590,7 +598,7 @@
             pltpu.VMEM((half, levels, 128), jnp.int32),
             pltpu.VMEM((levels, half, tiles + 1, 8, 128), BF16),
             pltpu.VMEM((levels, half, tiles + 1, 8, 128), BF16),
-            pltpu.VMEM((3 * windows + 1, 48, 256), BF16),
+            pltpu.VMEM((3 * windows + 1, 3, 8, 512), BF16),
             pltpu.VMEM((channels, 2 * channels), BF16),
             pltpu.VMEM((channels, channels), BF16),
             pltpu.VMEM((channels, channels), BF16),
@@ -609,10 +617,10 @@
             pltpu.SemaphoreType.DMA((6,)),
             pltpu.SemaphoreType.DMA((5,)),
             pltpu.SemaphoreType.DMA((5,)),
-            pltpu.SemaphoreType.DMA((rows // 16,)),
-            pltpu.SemaphoreType.DMA((rows // 16,)),
+            pltpu.SemaphoreType.DMA((windows // GROUP,)),
+            pltpu.SemaphoreType.DMA((windows // GROUP,)),
             pltpu.SemaphoreType.DMA((2,)),
-            pltpu.SemaphoreType.DMA((windows + 1,)),
+            pltpu.SemaphoreType.DMA((windows + 3,)),
             pltpu.SemaphoreType.DMA,
         ],
         compiler_params=pltpu.CompilerParams(
@@ -625,13 +633,13 @@
 def place(table, pieces, out):
     sources = pieces.shape[0]
     for group in range(sources // 8):
-        before = pieces[(8 * group + sources - 1) % sources, 0]
-        here = pieces[8 * group : 8 * group + 8, 0].reshape(384, 256)
+        before = pieces[(8 * group + sources - 1) % sources, 0].reshape(24, 512)
+        here = pieces[8 * group : 8 * group + 8, 0].reshape(192, 512)
         columns = dot(table[...], jnp.concatenate([before, here], 0)).astype(BF16)
         for lev in range(LEV):
-            for lanes in range(4):
-                at = (lev * 4 + lanes) * 48
-                out[lev, 0, 48 * group : 48 * group + 48, 256 * lanes : 256 * lanes + 256] = (
+            for lanes in range(2):
+                at = (lev * 2 + lanes) * 48
+                out[lev, 0, 48 * group : 48 * group + 48, 512 * lanes : 512 * lanes + 512] = (
                     columns[at : at + 48]
                 )
 
@@ -643,8 +651,8 @@
         grid=(3,),
         out_shape=jax.ShapeDtypeStruct((LEV, 3, n_lon * 6, 1024), BF16),
         in_specs=[
-            pl.BlockSpec((384, 432), lambda row: (0, 0)),
-            pl.BlockSpec((n_lon, 1, 48, 256), lambda row: (0, row, 0, 0)),
+            pl.BlockSpec((192, 216), lambda row: (0, 0)),
+            pl.BlockSpec((n_lon, 1, 3, 8, 512), lambda row: (0, row, 0, 0, 0)),
         ],
         out_specs=pl.BlockSpec((LEV, 1, n_lon * 6, 1024), lambda row: (0, row, 0, 0)),
         name="place_columns",

time: 110 us -> 105 us (0.955)
  Pallas kernels: 109 us -> 105 us
    pallas_call x1, Pallas kernels: 104 us -> 100 us  [exchange(): pl.pallas_call(functools.partial(fused, n_lat, n_lon), out_shape=jax.Shap...]
where the time goes in v3:
time: 105 us
  Pallas kernels  105 us (100%)
    pallas_call x1, Pallas kernels, exchange(): pl.pallas_call(functools.partial(fused, n_lat, n_lon), out_shape=jax.Shap...  100 us
    pallas_call x1, Pallas kernels, arrange(): pl.pallas_call(place, grid=(3,), out_shape=jax.ShapeDtypeStruct((LEV, 3,...  4.49 us

profile of v3, /device:TPU:0, one launch (start us, length us, event | category | flops | bytes accessed | tf_op | source)
XLA Modules:
  0.0 104.9 jit_solution(15686953248227579158)
XLA Ops:
  0.0 100.4 %attend_merge_send.1.pieces = bf16[32,3,3,8,512]{4,3,2,1,0:T(8,128)(2,1)} custom-call(bf16[2,12,24,8,512]{4,3,2,1,0:T(8,128)(2,1)} %bitcast.4, s32[12,2,192]{2,1,0:T(2,128)} %bitcast.5, bf16[4,144,384]{2,1,0:T(8,128)(2,1)} %constant.8.clone.pick, bf16[160,144]{1,0:T(8,128)(2,1)} %constant.9.clone.order, bf16[72,80]{1,0:T(8,128)(2,1)} %constant.10.clone.pack, ...), custom_call_target="tpu_custom_call" | custom-call | tf_op jit(solution)/shard_map/attend_merge_send/pallas_call | solution.py:587
  100.4 4.5 %place_columns.1 = bf16[2,3,192,1024]{3,2,1,0:T(8,128)(2,1)} custom-call(bf16[192,216]{1,0:T(8,128)(2,1)} %constant.11.clone.table, bf16[32,3,3,8,512]{4,3,2,1,0:T(8,128)(2,1)} %attend_merge_send.1.pieces), custom_call_target="tpu_custom_call" | custom-call | tf_op jit(solution)/shard_map/place_columns/pallas_call | solution.py:649

commit v4 on v3

--- a/solution.py
+++ b/solution.py
@@ -114,6 +114,9 @@
     odd_save,
     carry_send,
     carry_recv,
+    top_rows,
+    top_send,
+    top_recv,
     load_sems,
     row_send,
     row_recv,
@@ -135,7 +138,7 @@
     chunks = windows // GROUP
 
     def first_chunk(place):
-        return (place // 8) * (chunks // 4)
+        return place // 4
 
     first = first_chunk(lon)
     first_west = first_chunk(west_lon)
@@ -147,6 +150,7 @@
         pltpu.make_async_copy(w_qkv_hbm.at[:, 2 * channels :], w_v, load_sems.at[3]),
         pltpu.make_async_copy(w_out_hbm, w_out, load_sems.at[4]),
         pltpu.make_async_copy(w_merge_hbm, w_merge, load_sems.at[5]),
+        pltpu.make_async_copy(tokens.at[:, :, 0:1], top_rows, load_sems.at[6]),
     ]
     for load in loads:
         load.start()
@@ -208,7 +212,12 @@
         halo_case(lax.rem(first_west + step, chunks), first_west, lambda copy: copy.start())
         return 0
 
-    next_rows = pl.ds(rows // 8, 1)
+    line = lax.broadcasted_iota(jnp.int32, (40, 96), 0)
+    spot = lax.broadcasted_iota(jnp.int32, (40, 96), 1)
+    gather_top = (line // 3 * 8 + line % 3 == spot).astype(F32).astype(BF16)
+    spot = lax.broadcasted_iota(jnp.int32, (96, 40), 0)
+    line = lax.broadcasted_iota(jnp.int32, (96, 40), 1)
+    spread_top = (line // 3 * 8 + line % 3 == spot).astype(F32).astype(BF16)
     ahead = [
         remote(region.at[0:6], east_region, row_send.at[0], row_recv.at[0], (lat, west_lon)),
         remote(
@@ -222,15 +231,15 @@
             (prev_lat, west_lon),
         ),
         remote(
-            tokens.at[:, 6:12, 0:1],
-            own.at[:, :, next_rows],
+            top_send.at[0],
+            top_recv.at[0],
             row_send.at[3],
             row_recv.at[3],
             (prev_lat, lon),
         ),
         remote(
-            tokens.at[:, 0:6, 0:1],
-            east.at[:, :, next_rows],
+            top_send.at[1],
+            top_recv.at[1],
             row_send.at[4],
             row_recv.at[4],
             (prev_lat, west_lon),
@@ -238,10 +247,13 @@
     ]
     for copy in ahead[:3]:
         copy.start()
-    lax.fori_loop(0, 2, send_west, 0)
-    for copy in ahead[3:]:
-        copy.start()
-    lax.fori_loop(2, chunks, send_west, 0)
+    lax.fori_loop(0, 1, send_west, 0)
+    loads[6].wait()
+    for half in range(2):
+        top = top_rows[:, 6 - 6 * half : 12 - 6 * half].reshape(96, channels)
+        top_send[half] = dot(gather_top, top).astype(BF16).reshape(5, 8, channels)
+        ahead[3 + half].start()
+    lax.fori_loop(1, chunks, send_west, 0)
 
     def eye(size):
         row = lax.broadcasted_iota(jnp.int32, (size, size), 0)
@@ -433,6 +445,12 @@
         device_id_type=MESH,
     )
 
+    def finish_first(before, saved, place):
+        pieces = [before[16 * p : 16 * p + 16] for p in range(2)]
+        pieces += [odd_save[saved, pl.ds(16 * p, 16)] for p in range(2)]
+        merged = jnp.concatenate([merge(pieces), jnp.zeros((24, 2 * channels), F32)], 0)
+        stage[place] = packed(merged)[:24].reshape(3, 8, 512)
+
     carry[...] = jnp.zeros_like(carry)
     slot_row = lax.broadcasted_iota(jnp.int32, (GROUP * 40, 512), 0) % 40 < 12
 
@@ -444,8 +462,10 @@
 
         @pl.when(chunk == chunks - 1)
         def _():
-            ahead[3].wait_recv()
-            ahead[4].wait_recv()
+            for half, target in enumerate((own, east)):
+                ahead[3 + half].wait_recv()
+                top = dot(spread_top, top_recv[half].reshape(40, channels)).astype(BF16)
+                target[:, :, rows // 8] = top.reshape(LEV, 6, 8, channels)
 
         for i in range(GROUP):
             part = pl.ds(3 * chunk + PICK_STARTS[i], 2)
@@ -522,27 +542,28 @@
         def _():
             last_copy().start()
 
+        @pl.when(jnp.logical_and(step == chunks - 1, first != 0))
+        def _():
+            carry_copy.wait_recv()
+            finish_first(carry_recv[...].astype(F32), 0, 1)
+            part_of(0, 1, 1, 1, windows + 1)
+
         return 0
 
     lax.fori_loop(0, chunks, chunk_step, 0)
 
-    carry_copy.wait_recv()
-    lat_carry = carry_recv[...].astype(F32)
-    rows_of = lambda p: pl.ds(16 * p, 16)
-    pieces = [
-        jnp.concatenate([lat_carry[16 * p : 16 * p + 16], carry[pl.ds(40 * p, 16)]], 0)
-        for p in range(2)
-    ]
-    pieces += [jnp.concatenate([odd_save[0, rows_of(p)], odd_save[1, rows_of(p)]], 0) for p in range(2)]
-    merged = merge(pieces)
-    zero_rows = jnp.zeros((24, 2 * channels), F32)
-    stage[1] = packed(jnp.concatenate([merged[:16], zero_rows], 0))[:24].reshape(3, 8, 512)
-    part_of(0, 1, 1, 1, windows + 1)
+    @pl.when(first == 0)
+    def _():
+        carry_copy.wait_recv()
+        finish_first(carry_recv[...].astype(F32), 0, 1)
+        part_of(0, 1, 1, 1, windows + 1)
+
     split = GROUP * first
 
     @pl.when(first != 0)
     def _():
-        stage[3 * split + 1] = packed(jnp.concatenate([merged[16:], zero_rows], 0))[:24].reshape(3, 8, 512)
+        last = jnp.concatenate([carry[pl.ds(40 * p, 16)] for p in range(2)], 0)
+        finish_first(last, 1, 3 * split + 1)
         part_of(split, 3 * split, 0, 2, windows + 2)
 
     def wait_halo(chunk, _):
@@ -614,7 +635,10 @@
             pltpu.VMEM((2, 32, channels), F32),
             pltpu.VMEM((32, channels), BF16),
             pltpu.VMEM((32, channels), BF16),
-            pltpu.SemaphoreType.DMA((6,)),
+            pltpu.VMEM((levels, cols, 1, 8, channels), BF16),
+            pltpu.VMEM((2, 5, 8, channels), BF16),
+            pltpu.VMEM((2, 5, 8, channels), BF16),
+            pltpu.SemaphoreType.DMA((7,)),
             pltpu.SemaphoreType.DMA((5,)),
             pltpu.SemaphoreType.DMA((5,)),
             pltpu.SemaphoreType.DMA((windows // GROUP,)),

time: 105 us -> 101 us (0.962)
  Pallas kernels: 105 us -> 101 us
    pallas_call x1, Pallas kernels: 100 us -> 96.7 us  [exchange(): pl.pallas_call(functools.partial(fused, n_lat, n_lon), out_shape=jax.Shap...]
where the time goes in v4:
time: 101 us
  Pallas kernels  101 us (100%)
    pallas_call x1, Pallas kernels, exchange(): pl.pallas_call(functools.partial(fused, n_lat, n_lon), out_shape=jax.Shap...  96.7 us
    pallas_call x1, Pallas kernels, arrange(): pl.pallas_call(place, grid=(3,), out_shape=jax.ShapeDtypeStruct((LEV, 3,...  4.49 us

profile of v4, /device:TPU:0, one launch (start us, length us, event | category | flops | bytes accessed | tf_op | source)
XLA Modules:
  0.0 101.2 jit_solution(12655622368956043862)
XLA Ops:
  0.0 96.7 %attend_merge_send.1.pieces = bf16[32,3,3,8,512]{4,3,2,1,0:T(8,128)(2,1)} custom-call(bf16[2,12,24,8,512]{4,3,2,1,0:T(8,128)(2,1)} %bitcast.4, s32[12,2,192]{2,1,0:T(2,128)} %bitcast.5, bf16[4,144,384]{2,1,0:T(8,128)(2,1)} %constant.8.clone.pick, bf16[160,144]{1,0:T(8,128)(2,1)} %constant.9.clone.order, bf16[72,80]{1,0:T(8,128)(2,1)} %constant.10.clone.pack, ...), custom_call_target="tpu_custom_call" | custom-call | tf_op jit(solution)/shard_map/attend_merge_send/pallas_call | solution.py:608
  96.7 4.5 %place_columns.1 = bf16[2,3,192,1024]{3,2,1,0:T(8,128)(2,1)} custom-call(bf16[192,216]{1,0:T(8,128)(2,1)} %constant.11.clone.table, bf16[32,3,3,8,512]{4,3,2,1,0:T(8,128)(2,1)} %attend_merge_send.1.pieces), custom_call_target="tpu_custom_call" | custom-call | tf_op jit(solution)/shard_map/place_columns/pallas_call | solution.py:673

commit v5 on v4

--- a/solution.py
+++ b/solution.py
@@ -152,9 +152,6 @@
         pltpu.make_async_copy(w_merge_hbm, w_merge, load_sems.at[5]),
         pltpu.make_async_copy(tokens.at[:, :, 0:1], top_rows, load_sems.at[6]),
     ]
-    for load in loads:
-        load.start()
-
     barrier = pltpu.get_barrier_semaphore()
 
     def greet(step, _):
@@ -174,6 +171,9 @@
             return 0
 
         lax.fori_loop(0, n_lon, greet_before, 0)
+
+    for load in loads:
+        load.start()
 
     pl.semaphore_wait(barrier, n_lon + 3)
 
@@ -660,25 +660,23 @@
         before = pieces[(8 * group + sources - 1) % sources, 0].reshape(24, 512)
         here = pieces[8 * group : 8 * group + 8, 0].reshape(192, 512)
         columns = dot(table[...], jnp.concatenate([before, here], 0)).astype(BF16)
-        for lev in range(LEV):
-            for lanes in range(2):
-                at = (lev * 2 + lanes) * 48
-                out[lev, 0, 48 * group : 48 * group + 48, 512 * lanes : 512 * lanes + 512] = (
-                    columns[at : at + 48]
-                )
+        for lanes in range(2):
+            out[0, 0, 48 * group : 48 * group + 48, 512 * lanes : 512 * lanes + 512] = columns[
+                48 * lanes : 48 * lanes + 48
+            ]
 
 
 def arrange(recv):
     n_lon = recv.shape[0]
     return pl.pallas_call(
         place,
-        grid=(3,),
+        grid=(3, LEV),
         out_shape=jax.ShapeDtypeStruct((LEV, 3, n_lon * 6, 1024), BF16),
         in_specs=[
-            pl.BlockSpec((192, 216), lambda row: (0, 0)),
-            pl.BlockSpec((n_lon, 1, 3, 8, 512), lambda row: (0, row, 0, 0, 0)),
+            pl.BlockSpec((96, 216), lambda row, lev: (lev, 0)),
+            pl.BlockSpec((n_lon, 1, 3, 8, 512), lambda row, lev: (0, row, 0, 0, 0)),
         ],
-        out_specs=pl.BlockSpec((LEV, 1, n_lon * 6, 1024), lambda row: (0, row, 0, 0)),
+        out_specs=pl.BlockSpec((1, 1, n_lon * 6, 1024), lambda row, lev: (lev, row, 0, 0)),
         name="place_columns",
     )(arrange_table(), recv)
 

time: 101 us -> 103 us (1.020)
  Pallas kernels: 101 us -> 103 us
    pallas_call x1, Pallas kernels: 4.49 us -> 6.06 us  [arrange(): pl.pallas_call(place, grid=(3, LEV), out_shape=jax.ShapeDtypeStruct((LEV,...]
where the time goes in v5:
time: 103 us
  Pallas kernels  103 us (100%)
    pallas_call x1, Pallas kernels, exchange(): pl.pallas_call(functools.partial(fused, n_lat, n_lon), out_shape=jax.Shap...  96.5 us
    pallas_call x1, Pallas kernels, arrange(): pl.pallas_call(place, grid=(3, LEV), out_shape=jax.ShapeDtypeStruct((LEV,...  6.06 us

profile of v5, /device:TPU:0, one launch (start us, length us, event | category | flops | bytes accessed | tf_op | source)
XLA Modules:
  0.0 102.5 jit_solution(13159999928876317203)
XLA Ops:
  0.0 96.5 %attend_merge_send.1.pieces = bf16[32,3,3,8,512]{4,3,2,1,0:T(8,128)(2,1)} custom-call(bf16[2,12,24,8,512]{4,3,2,1,0:T(8,128)(2,1)} %bitcast.4, s32[12,2,192]{2,1,0:T(2,128)} %bitcast.5, bf16[4,144,384]{2,1,0:T(8,128)(2,1)} %constant.8.clone.pick, bf16[160,144]{1,0:T(8,128)(2,1)} %constant.9.clone.order, bf16[72,80]{1,0:T(8,128)(2,1)} %constant.10.clone.pack, ...), custom_call_target="tpu_custom_call" | custom-call | tf_op jit(solution)/shard_map/attend_merge_send/pallas_call | solution.py:608
  96.5 6.1 %place_columns.1 = bf16[2,3,192,1024]{3,2,1,0:T(8,128)(2,1)} custom-call(bf16[192,216]{1,0:T(8,128)(2,1)} %constant.11.clone.table, bf16[32,3,3,8,512]{4,3,2,1,0:T(8,128)(2,1)} %attend_merge_send.1.pieces), custom_call_target="tpu_custom_call" | custom-call | tf_op jit(solution)/shard_map/place_columns/pallas_call | solution.py:671
